TPU v7x, 1024 devices: a whole 8x8x8 slice. The times are simulated.
1024 devices in a mesh: patch: 32 (over y, z_hi, core), det: 32 (over x, z_lo).
Axes of the slice: x: 8, y: 8, z: 8 (z_hi: 2, z_lo: 4; z = z_hi * 4 + z_lo), core: 2. Of those that a mesh axis runs over, the one named last changes fastest.
Arguments:
- tod_image: float32 [32, 32, 128, 1024], P('patch', 'det'), may hold values from -6 to 6
- angles: float32 [32, 32, 128, 1024], P('patch', 'det'), may hold values from -3.140625 to 3.140625
- pixel_offset: int32 [32, 32, 128, 1024], P('patch', 'det'), may hold values from 0 to 63
- target_patch: int32 [32, 32, 128, 1], P('patch', 'det'), may hold values from 0 to 31; in each aligned block of 128 rows (0 to 127, 128 to 255, ..., all dimensions but the last counted through in order) at most 8 rows name the same one
- target_block: int32 [32, 32, 128], P('patch', 'det'), may hold values from 0 to 255
- noise_spectrum: float32 [32, 32, 4, 513], P('patch', 'det'), may hold values from 0.1 to 1
- residual: float32 [32, 256, 3, 64], P('patch', 'det'), may hold values from -6 to 6
- previous_rz: float32 [1], replicated, may hold values from 2097152 to 33554432
- legendre: float32 [128, 64, 64], P('det'), may hold values from -0.75 to 0.75
- harmonic_filter: float32 [128, 64], P('det'), may hold values from 0.53333336 to 10.666667
Outputs:
- new_residual: float32 [32, 256, 3, 64], P('patch', 'det')
- preconditioned: float32 [32, 128, 6, 64], P('patch', 'det')
- beta: float32 [1], replicated
Inputs may be any that keep to these rules, and one draw needn't show every extreme that they name: `target_patch`: among the 128 blocks of one device at most 8 name the same patch, a bound that some device reaches.
All inputs are finite; a program needn't handle non-finite values.
Results may differ from a plain program's by a relative error of at most 0.0003.
Values sent between devices are 32-bit elements; how exact they have to be, the bound alone decides.
A program may use at most 32 MiB of HBM per device.

v0:
```python
import math

import jax
import jax.numpy as jnp
from jax import lax
from jax.sharding import PartitionSpec as P

NPHI = 256


PRECISE = lax.Precision.HIGHEST


def fourier_tables(length, first_mode, mode_count):
    sample_index = lax.broadcasted_iota(jnp.int32, (length, mode_count), 0)
    mode_index = lax.broadcasted_iota(jnp.int32, (length, mode_count), 1) + first_mode
    phase_angle = (sample_index * mode_index % length).astype(jnp.float32) * (
        2.0 * math.pi / length
    )
    return (jnp.cos(phase_angle), jnp.sin(phase_angle))


def weight_noise(samples, spectrum):
    length = samples.shape[1]
    half_count = length // 2 + 1
    cos_table, sin_table = fourier_tables(length, 0, half_count)
    cos_part = jnp.dot(samples, cos_table, precision=PRECISE)
    sin_part = jnp.dot(samples, sin_table, precision=PRECISE)
    freq_index = lax.broadcasted_iota(jnp.int32, (1, half_count), 1)
    edge_weights = jnp.where((freq_index == 0) | (freq_index == length // 2), 1.0, 2.0) / length
    per_block = jnp.repeat(spectrum, samples.shape[0] // spectrum.shape[0], axis=0) * edge_weights
    return jnp.dot(cos_part * per_block, cos_table.T, precision=PRECISE) + jnp.dot(
        sin_part * per_block, sin_table.T, precision=PRECISE
    )


def bin_blocks(filtered, angle_rows, offsets, pixel_count):
    block_count, length = filtered.shape
    weighted = jnp.stack(
        [filtered, filtered * jnp.cos(2.0 * angle_rows), filtered * jnp.sin(2.0 * angle_rows)],
        axis=1,
    )
    grouped = weighted.reshape(block_count // 16, 16, 3, length)
    grouped_offsets = offsets.reshape(block_count // 16, 16, length)
    pixel_index = lax.broadcasted_iota(jnp.int32, (1, 1, pixel_count), 2)

    def one_group(group_pair):
        values, places = group_pair
        onehot = (places[:, :, None] == pixel_index).astype(jnp.float32)
        return jnp.einsum("gst,gtk->gsk", values, onehot, precision=PRECISE)

    binned = lax.map(one_group, (grouped, grouped_offsets))
    return binned.reshape(block_count, 3 * pixel_count)


def cycle_coefficients(fields, legendre):
    stacks, local_rows, components, pixel_count = fields.shape
    cycles_here = local_rows * pixel_count // NPHI
    along_cycle = fields.reshape(stacks, cycles_here, NPHI // pixel_count, components, pixel_count)
    along_cycle = along_cycle.transpose(0, 1, 3, 2, 4).reshape(
        stacks, cycles_here, components, NPHI
    )
    modes_here = legendre.shape[0]
    own_first = lax.axis_index("det") * modes_here
    cycle_piece = lax.all_gather(along_cycle, "det", axis=1, tiled=True)
    cos_table, sin_table = fourier_tables(NPHI, own_first, modes_here)
    cos_part = jnp.einsum("krsp,pm->krms", cycle_piece, cos_table, precision=PRECISE)
    sin_part = jnp.einsum("krsp,pm->krms", cycle_piece, sin_table, precision=PRECISE)
    paired = jnp.stack([cos_part, sin_part], axis=-1)
    columns = paired.reshape(
        cycle_piece.shape[0], cycle_piece.shape[1], modes_here, 2 * components
    ) * math.sqrt(2.0 / NPHI)
    return jnp.einsum("mlr,krmc->kmcl", legendre, columns, precision=PRECISE)


def per_device(
    tod_image,
    angles,
    pixel_offset,
    target_patch,
    target_block,
    noise_spectrum,
    residual,
    previous_rz,
    legendre,
    harmonic_filter,
):
    samples = tod_image[0, 0]
    filtered = weight_noise(samples, noise_spectrum[0, 0])
    local_curvature = jnp.sum(samples * filtered)
    pixel_count = residual.shape[3]
    local_rows = residual.shape[1]
    binned = bin_blocks(filtered, angles[0, 0], pixel_offset[0, 0], pixel_count)
    destinations = target_patch[0, 0, :, 0]
    blocks_here = target_block[0, 0]
    block_count = binned.shape[0]
    patches = lax.axis_size("patch")
    capacity = 2 * block_count // patches
    patch_index = lax.broadcasted_iota(jnp.int32, (1, patches), 1)
    matches = (destinations[:, None] == patch_index).astype(jnp.int32)
    running = jnp.cumsum(matches, axis=0) - 1
    slot_index = jnp.sum(running * matches, axis=1)
    position = destinations * capacity + slot_index
    slot_rows = lax.broadcasted_iota(jnp.int32, (patches * capacity, 1), 0)
    select = (position[None, :] == slot_rows).astype(jnp.float32)
    payload = jnp.dot(select, binned, precision=PRECISE)
    labels = jnp.dot(select, (blocks_here + 1).astype(jnp.float32), precision=PRECISE) - 1.0
    received, received_labels = (
        lax.all_to_all(
            payload.reshape(patches, capacity, 3 * pixel_count),
            "patch",
            split_axis=0,
            concat_axis=0,
            tiled=True,
        ),
        lax.all_to_all(
            labels.reshape(patches, capacity), "patch", split_axis=0, concat_axis=0, tiled=True
        ),
    )
    flat_payload = received.reshape(patches * capacity, 3 * pixel_count)
    flat_labels = received_labels.reshape(1, patches * capacity)
    target = lax.broadcasted_iota(jnp.int32, (local_rows * lax.axis_size("det"), 1), 0).astype(
        jnp.float32
    )
    onehot = (flat_labels == target).astype(jnp.float32)
    mapped = lax.psum_scatter(
        jnp.dot(onehot, flat_payload, precision=PRECISE), "det", scatter_dimension=0, tiled=True
    )
    mapped = mapped.reshape(residual.shape)
    rz_before = previous_rz[0]
    curvature = lax.psum(local_curvature, ("patch", "det"))
    step_size = rz_before / curvature
    new_residual = residual - step_size * mapped
    coefficients = cycle_coefficients(new_residual, legendre)[0]
    preconditioned = harmonic_filter[:, None, :] * coefficients
    rz_after = lax.psum(jnp.sum(preconditioned * coefficients), ("patch", "det"))
    beta = jnp.reshape(rz_after / rz_before, (1,))
    return (new_residual, preconditioned[None], beta)


def solution(mesh):
    placed = (
        P("patch", "det", None, None),
        P("patch", "det", None, None),
        P("patch", "det", None, None),
        P("patch", "det", None, None),
        P("patch", "det", None),
        P("patch", "det", None, None),
        P("patch", "det", None, None),
        P(),
        P("det", None, None),
        P("det", None),
    )
    return jax.shard_map(
        per_device,
        mesh=mesh,
        in_specs=placed,
        out_specs=(P("patch", "det", None, None), P("patch", "det", None, None), P()),
        check_vma=False,
    )
```

profile of v0, /device:TPU:1, one launch (start us, length us, event | category | flops | bytes accessed | tf_op | source)
XLA Modules:
  0.0 507.4 jit_solution(18000286799686671774)
XLA Ops:
  11.2 21.3 %all-to-all-start = ((f32[32,1,8]{2,1,0:T(1,128)}), f32[32,1,8]{2,1,0:T(1,128)S(1)}, u32[]{:S(2)}, u32[]{:S(2)}) async-start(f32[32,1,8]{2,1,0:T(1,128)} %bitcast.10), calls=%async_computation | async-start | bytes 32768 | tf_op jit(solution)/shard_map/all_to_all | solution.py:116
  33.4 15.1 %fusion.34 = f32[128,513]{0,1:T(8,128)S(1)} fusion(f32[1,1,128,1024]{3,2,1,0:T(8,128)} %param.12, f32[128,513]{0,1:T(8,128)S(1)} %copy.30, f32[513]{0:T(1024)S(1)} %select_multiply_fusion), kind=kOutput, calls=%fused_computation.29 | convolution fusion | flops 814364928 | bytes 1051652 | tf_op jit(solution)/shard_map/dot_general | solution.py:27
  48.5 13.8 %fusion.37 = f32[128,513]{0,1:T(8,128)S(1)} fusion(f32[1,1,128,1024]{3,2,1,0:T(8,128)S(1)} %copy-done.4, f32[128,513]{0,1:T(8,128)S(1)} %copy.30, f32[513]{0:T(1024)S(1)} %select_multiply_fusion), kind=kOutput, calls=%fused_computation.30 | convolution fusion | flops 814364928 | bytes 1051652 | tf_op jit(solution)/shard_map/dot_general | solution.py:28
  62.3 12.9 %fusion.17 = f32[128,1024]{1,0:T(8,128)S(1)} fusion(f32[128,513]{0,1:T(8,128)S(1)} %fusion.34), kind=kOutput, calls=%fused_computation.22 | convolution fusion | flops 814233600 | bytes 786944 | tf_op jit(solution)/shard_map/dot_general | solution.py:32
  75.2 15.2 %bitcast_multiply_fusion.1 = (f32[128,1024]{1,0:T(8,128)S(1)}, f32[128,1024]{1,0:T(8,128)S(1)}, f32[]{:T(128)}, f32[128,1024]{1,0:T(8,128)S(1)}) fusion(f32[1,1,128,1024]{3,2,1,0:T(8,128)S(1)} %copy-done.3, f32[1,1,128,1024]{3,2,1,0:T(8,128)S(1)} %copy-done.4, f32[128,1024]{1,0:T(8,128)S(1)} %fusion.17, f32[128,513]{0,1:T(8,128)S(1)} %fusion.37), kind=kOutput, calls=%fused_computation.34 | convolution fusion | flops 815020032 | bytes 3408388 | tf_op jit(solution)/shard_map/dot_general | solution.py:32
  92.0 1.4 pad_maximum_fusion
  93.4 22.9 %while.11 = (s32[]{:T(128)}, f32[8,16,3,64]{3,2,1,0:T(4,128)S(1)}, f32[8,16,3,1024]{3,2,1,0:T(4,128)S(1)}, s32[8,16,1024]{2,1,0:T(8,128)}, s32[]{:T(128)}) while((s32[]{:T(128)}, f32[8,16,3,64]{3,2,1,0:T(4,128)S(1)}, f32[8,16,3,1024]{3,2,1,0:T(4,128)S(1)}, s32[8,16,1024]{2,1,0:T(8,128)}, s32[]{:T(128)}) %tuple.37), condition=%wide.region_5.6_spmd.clone, body=%wide.region_4.5_spmd.clone.sunk | while | flops 38797312 | bytes 492609 | solution.py:52
  93.4 0.8 dynamic-slice_bitcast_fusion.2
  94.3 2.0 fusion.110
  96.3 0.9 dynamic-slice_bitcast_fusion.2
  97.2 2.0 fusion.110
  99.2 0.9 dynamic-slice_bitcast_fusion.2
  100.0 2.0 fusion.110
  102.0 0.9 dynamic-slice_bitcast_fusion.2
  102.9 2.0 fusion.110
  104.9 0.9 dynamic-slice_bitcast_fusion.2
  105.8 2.0 fusion.110
  107.8 0.9 dynamic-slice_bitcast_fusion.2
  108.6 2.0 fusion.110
  110.6 0.9 dynamic-slice_bitcast_fusion.2
  111.5 2.0 fusion.110
  113.5 0.9 dynamic-slice_bitcast_fusion.2
  114.4 2.0 fusion.110
  116.6 1.0 fusion.50
  117.6 12.2 %all-to-all-start.1 = ((f32[32,8,192]{2,1,0:T(8,128)}), f32[32,8,192]{2,1,0:T(8,128)S(1)}, u32[]{:S(2)}, u32[]{:S(2)}) async-start(f32[32,8,192]{2,1,0:T(8,128)} %fusion.50), calls=%async_computation.1 | async-start | bytes 524288 | tf_op jit(solution)/shard_map/all_to_all | solution.py:109
  131.1 14.0 %all-to-all-done.1 = f32[32,8,192]{2,1,0:T(8,128)S(1)} async-done(((f32[32,8,192]{2,1,0:T(8,128)}), f32[32,8,192]{2,1,0:T(8,128)S(1)}, u32[]{:S(2)}, u32[]{:S(2)}) %all-to-all-start.1) | async-done | bytes 196640 | tf_op jit(solution)/shard_map/all_to_all | solution.py:109
  145.1 1.0 fusion.43
  146.1 116.2 %psum.14 = f32[]{:T(128)} all-reduce(f32[]{:T(128)} %get-tuple-element.60), channel_id=1, replica_groups=mesh['patch'=32,'det'=32] {'patch','det'}, use_global_device_ids=true, to_apply=%region_1.2 | all-reduce | flops 1 | bytes 8 | tf_op jit(solution)/shard_map/psum | solution.py:131
  263.7 18.1 %reduce-scatter.2.cloned.1.call-done = f32[8,192]{1,0:T(8,128)} async-done(((f32[256,192]{1,0:T(8,128)}), f32[8,192]{1,0:T(8,128)}) %reduce-scatter.2.cloned.1.call-update) | async-done | bytes 6160 | tf_op jit(solution)/shard_map/reduce_scatter | solution.py:126
  282.6 60.8 %all_gather.3 = f32[1,64,3,256]{3,0,2,1:T(1,128)S(1)} all-gather(f32[1,2,3,256]{3,0,2,1:T(1,128)S(1)} %reshape.131), channel_id=1, replica_groups=mesh['patch'=32,'det'=32] {'det'}, dimensions={1}, use_global_device_ids=true | all-gather | bytes 202752 | tf_op jit(solution)/shard_map/all_gather | solution.py:65
  344.9 0.9 fusion.60
  345.8 152.1 %psum.15 = f32[]{:T(128)} all-reduce(f32[]{:T(128)} %get-tuple-element.61), channel_id=1, replica_groups=mesh['patch'=32,'det'=32] {'patch','det'}, use_global_device_ids=true, to_apply=%region_8.9 | all-reduce | flops 1 | bytes 8 | tf_op jit(solution)/shard_map/psum | solution.py:136
  (45 shorter events, 10.9 us)
Async XLA Ops:
  7.2 337.7 %copy-start = (f32[4,64,64]{2,1,0:T(8,128)S(1)}, f32[4,64,64]{2,1,0:T(8,128)}, u32[]{:S(2)}) copy-start(f32[4,64,64]{2,1,0:T(8,128)} %param.20) | copy-start | bytes 196612
  11.2 106.4 %all-to-all-start = ((f32[32,1,8]{2,1,0:T(1,128)}), f32[32,1,8]{2,1,0:T(1,128)S(1)}, u32[]{:S(2)}, u32[]{:S(2)}) async-start(f32[32,1,8]{2,1,0:T(1,128)} %bitcast.10), calls=%async_computation | async-start | bytes 32768 | tf_op jit(solution)/shard_map/all_to_all | solution.py:116
  33.3 15.1 %copy-start.4 = (f32[1,1,128,1024]{3,2,1,0:T(8,128)S(1)}, f32[1,1,128,1024]{3,2,1,0:T(8,128)}, u32[]{:S(2)}) copy-start(f32[1,1,128,1024]{3,2,1,0:T(8,128)} %param.12) | copy-start | bytes 1572868
  62.2 12.9 %copy-start.3 = (f32[1,1,128,1024]{3,2,1,0:T(8,128)S(1)}, f32[1,1,128,1024]{3,2,1,0:T(8,128)}, u32[]{:S(2)}) copy-start(f32[1,1,128,1024]{3,2,1,0:T(8,128)} %param.13) | copy-start | bytes 1572868
  116.4 166.2 %copy-start.1 = (f32[1,8,3,64]{3,1,2,0:T(8,128)S(1)}, f32[1,8,3,64]{3,1,2,0:T(8,128)}, u32[]{:S(2)}) copy-start(f32[1,8,3,64]{3,1,2,0:T(8,128)} %param.18) | copy-start | bytes 18436
  116.4 228.5 %copy-start.2 = (f32[4,64]{1,0:T(4,128)S(1)}, f32[4,64]{1,0:T(4,128)}, u32[]{:S(2)}) copy-start(f32[4,64]{1,0:T(4,128)} %param.21) | copy-start | bytes 3076
  117.6 27.5 %all-to-all-start.1 = ((f32[32,8,192]{2,1,0:T(8,128)}), f32[32,8,192]{2,1,0:T(8,128)S(1)}, u32[]{:S(2)}, u32[]{:S(2)}) async-start(f32[32,8,192]{2,1,0:T(8,128)} %fusion.50), calls=%async_computation.1 | async-start | bytes 524288 | tf_op jit(solution)/shard_map/all_to_all | solution.py:109
  129.8 152.0 %reduce-scatter.2.cloned.1.call-start = ((), (), s32[]{:S(2)}) async-start(), calls=%async_computation.3 | async-start | bytes 270336 | tf_op jit(solution)/shard_map/reduce_scatter | solution.py:126
Sparse Core Ops, SparseCore 0:
  146.3 135.4 reduce-scatter.1
where the time goes:
time: 517 us; the launch traced here: 507 us
  blocking collectives  329 us (64%)
  matrix products  77.4 us (15%)
  starting transfers between devices  33.5 us (6%)
  waiting for transfers between devices  32.1 us (6%)
  between operations  17.6 us (3%)
  local copies, waits for them, and re-layouts  12.3 us (2%)
  other arithmetic  5.29 us (1%)
    psum x1, blocking collectives, per_device(): lax.psum(jnp.sum(preconditioned * coefficients), ('patch', 'det'))  152 us
    psum x1, blocking collectives, per_device(): curvature = lax.psum(local_curvature, ('patch', 'det'))  116 us
    all_gather x1, blocking collectives, cycle_coefficients(): cycle_piece = lax.all_gather(along_cycle, 'det', axis=1, tiled=True)  60.8 us
    all_to_all x1, starting transfers between devices, per_device(): lax.all_to_all(labels.reshape(patches, capacity), 'patch', split_axis=0,...  21.3 us
    reduce_scatter x1, waiting for transfers between devices, per_device(): lax.psum_scatter(jnp.dot(onehot, flat_payload, precision=PRECISE), 'det',...  18.1 us
    dot_general x8, matrix products, one_group(): return jnp.einsum('gst,gtk->gsk', values, onehot, precision=PRECISE)  16.1 us
    dot_general x1, matrix products, weight_noise(): jnp.dot(sin_part * per_block, sin_table.T, precision=PRECISE)  15.2 us
    dot_general x1, matrix products, weight_noise(): cos_part = jnp.dot(samples, cos_table, precision=PRECISE)  15.1 us
  transfers between devices with their start and end apart: 3, of which 2 were waited for; matrix products, arithmetic and copies ran while one was open for 17% of the time, Pallas kernels for 0%

commit v1 on v0

v1 whole, which is shorter than its diff:
```python
import functools
import math

import jax
import jax.numpy as jnp
import numpy as np
from jax import lax
from jax.experimental import pallas as pl
from jax.experimental.pallas import tpu as pltpu
from jax.sharding import PartitionSpec as P

BF16 = jnp.bfloat16
F32 = jnp.float32
I32 = jnp.int32
MESH = pl.DeviceIdType.MESH
LANES = 128
RADIX = 8
GROUP = 16
HIGH = 4
LOW = 16
LABEL_LANE = 12
CURVE_LANE = 13
ROOT_HALF = math.sqrt(0.5)


def split2(x):
    hi = x.astype(BF16)
    return hi, (x - hi.astype(F32)).astype(BF16)


def split3(x):
    hi = x.astype(BF16)
    rest = x - hi.astype(F32)
    mid = rest.astype(BF16)
    return hi, mid, (rest - mid.astype(F32)).astype(BF16)


def dot(a, b):
    return lax.dot_general(a, b, (((1,), (0,)), ((), ())), preferred_element_type=F32)


def dot_nt(a, b):
    return lax.dot_general(a, b, (((1,), (1,)), ((), ())), preferred_element_type=F32)


def iota(shape, dim):
    return lax.broadcasted_iota(I32, shape, dim)


def np_split_rows(table):
    hi = table.astype(np.float32).astype(BF16)
    lo = (table - hi.astype(np.float64)).astype(np.float32).astype(BF16)
    return np.concatenate([hi, hi, lo], axis=0)


def fourier_matrix():
    j = np.arange(LANES)
    angle = 2.0 * np.pi * (np.outer(j, j) % LANES) / LANES
    c, s = np.cos(angle), np.sin(angle)
    return np_split_rows(np.block([[c, -s], [s, c]]))


def twiddle_rows():
    n = np.arange(LANES)
    angle = [2.0 * np.pi * n * k / (RADIX * LANES) for k in range(1, 5)]
    return np.stack([np.cos(a) for a in angle] + [np.sin(a) for a in angle]).astype(np.float32)


def cycle_matrix(modes_here):
    f = np.arange(256)[:, None]
    lane = np.arange(LANES)
    mode = (-(lane // modes_here) % (LANES // modes_here)) * modes_here + lane % modes_here
    angle = 2.0 * np.pi * (f * mode % 256) / 256.0
    scale = math.sqrt(2.0 / 256.0)
    return np_split_rows(np.concatenate([np.cos(angle), np.sin(angle)], axis=1) * scale)


def pixel_spread():
    col = np.arange(3 * 256)
    s, pixel = col // 256, col % 64
    a, c = pixel // LOW, pixel % LOW
    source = (c // 8) * LANES + (c % 8) * 16 + s * HIGH + a
    return (np.arange(256)[:, None] == source).astype(np.float32).astype(BF16)


def double_angle(theta):
    n = jnp.round(theta * (2.0 / math.pi))
    odd = (n.astype(I32) & 1) == 1
    hi = np.float32(math.pi / 2)
    lo = np.float32(math.pi / 2 - float(hi))
    r = (theta - n * hi) - n * lo
    y = r * r
    c = jnp.full_like(y, COS_POLY[-1])
    for coef in COS_POLY[-2::-1]:
        c = c * y + coef
    s = jnp.full_like(y, SIN_POLY[-1])
    for coef in SIN_POLY[-2::-1]:
        s = s * y + coef
    return odd, c, s * r


def fit_polys():
    top = (math.pi / 4) ** 2 * 1.0001
    y = top * 0.5 * (1.0 - np.cos(np.pi * (np.arange(400) + 0.5) / 400))
    r = np.sqrt(y)
    power = y[:, None] ** np.arange(6)
    cos_c = np.linalg.lstsq(power, np.cos(2 * r), rcond=None)[0]
    sin_c = np.linalg.lstsq(power[:, :5], np.sin(2 * r) / r, rcond=None)[0]
    return [float(np.float32(v)) for v in cos_c], [float(np.float32(v)) for v in sin_c]


COS_POLY, SIN_POLY = fit_polys()


def filter_blocks(x, spec_ref, table, tw):
    blocks = x.shape[0]
    dets = spec_ref.shape[0]
    t = [x[:, i * LANES : (i + 1) * LANES] for i in range(RADIX)]
    a = [t[i] + t[i + 4] for i in range(4)]
    b = [t[i] - t[i + 4] for i in range(4)]
    even, odd = a[0] + a[2], a[1] + a[3]
    diff, both = (b[1] - b[3]) * ROOT_HALF, (b[1] + b[3]) * ROOT_HALF
    y = [
        (even + odd, None),
        (b[0] + diff, -(b[2] + both)),
        (a[0] - a[2], a[3] - a[1]),
        (b[0] - diff, b[2] - both),
        (even - odd, None),
    ]
    rows = [jnp.concatenate([y[0][0], jnp.zeros_like(x[:, :LANES])], axis=1)]
    for k in range(1, 5):
        c, s = tw[k - 1 : k, :], tw[k + 3 : k + 4, :]
        re, im = y[k]
        if im is None:
            rows.append(jnp.concatenate([re * c, -(re * s)], axis=1))
        else:
            rows.append(jnp.concatenate([re * c + im * s, im * c - re * s], axis=1))
    hi, lo = split2(jnp.concatenate(rows, axis=0))
    spectrum = dot(jnp.concatenate([hi, lo, hi], axis=1), table)

    col = iota((1, 5 * LANES), 1)
    k_of, j_of = col // LANES, col % LANES
    order = k_of + RADIX * j_of
    place = jnp.minimum(order, RADIX * LANES - order)
    pick = (iota((512, 5 * LANES), 0) == place).astype(F32).astype(BF16)
    own = spec_ref[...]
    parts = split3(own[:, :512])
    weight = dot(parts[0], pick) + dot(parts[1], pick) + dot(parts[2], pick)
    weight = weight + jnp.where(place == 512, own[:, 512:513], 0.0)
    edge = (k_of == 0) | (k_of == 4)
    weight = weight * jnp.where(edge, 1.0 / 1024.0, 2.0 / 1024.0)

    per = blocks // dets
    scaled = []
    for k in range(5):
        w = weight[:, k * LANES : (k + 1) * LANES]
        w = jnp.concatenate([w, -w], axis=1)
        for d in range(dets):
            part = spectrum[k * blocks + d * per : k * blocks + (d + 1) * per, :]
            scaled.append(part * w[d : d + 1, :])
    hi, lo = split2(jnp.concatenate(scaled, axis=0))
    u = dot(jnp.concatenate([hi, lo, hi], axis=1), table)
    re = [u[k * blocks : (k + 1) * blocks, :LANES] for k in range(5)]
    im = [u[k * blocks : (k + 1) * blocks, LANES:] for k in range(5)]
    tr, ti = [re[0]], [None]
    for k in range(1, 5):
        c, s = tw[k - 1 : k, :], tw[k + 3 : k + 4, :]
        tr.append(re[k] * c + im[k] * s)
        ti.append(re[k] * s - im[k] * c)
    plus, minus = tr[0] + tr[4], tr[0] - tr[4]
    p1, m1 = (tr[1] + ti[1]) * ROOT_HALF, (tr[1] - ti[1]) * ROOT_HALF
    p3, m3 = (tr[3] + ti[3]) * ROOT_HALF, (tr[3] - ti[3]) * ROOT_HALF
    e0, e1 = plus + tr[2], tr[1] + tr[3]
    f0, f1 = plus - tr[2], ti[3] - ti[1]
    g0, g1 = minus - ti[2], m1 - p3
    h0, h1 = minus + ti[2], m3 - p1
    return [e0 + e1, g0 + g1, f0 + f1, h0 + h1, e0 - e1, g0 - g1, f0 - f1, h0 - h1]


def local_kernel(
    patches, x_ref, angle_ref, offset_ref, patch_ref, block_ref, spec_ref, table_ref, tw_ref,
    out_ref, val_ref, low_ref, high_ref, binned_ref,
):
    blocks, length = x_ref.shape
    x = x_ref[...]
    filtered = filter_blocks(x, spec_ref, table_ref[...], tw_ref[...])
    total = jnp.zeros((blocks, LANES), F32)
    for i in range(RADIX):
        at = slice(i * LANES, (i + 1) * LANES)
        f = filtered[i]
        total = total + x[:, at] * f
        odd, c, s = double_angle(angle_ref[:, at])
        turned = jnp.where(odd, -f, f)
        for comp, v in enumerate((f, turned * c, turned * s)):
            hi, lo = split2(v)
            val_ref[comp, :, at] = hi
            val_ref[3 + comp, :, at] = lo
        off = offset_ref[:, at]
        low_ref[:, at] = (off & (LOW - 1)).astype(F32).astype(BF16)
        high_ref[:, at] = (off >> 4).astype(F32).astype(BF16)
    curvature = jnp.sum(jnp.sum(total, axis=0, keepdims=True), axis=1, keepdims=True)

    lane = iota((GROUP, LANES), 1) % 16

    def one_group(g, carry):
        rows = pl.ds(pl.multiple_of(g * GROUP, GROUP), GROUP)
        low, high = low_ref[rows, :], high_ref[rows, :]
        ones = jnp.concatenate(
            [jnp.where(low == k, 1.0, 0.0).astype(BF16) for k in range(LOW)], axis=0
        )
        masks = [high == k for k in range(HIGH)]
        values = []
        for comp in range(6):
            v = val_ref[comp, rows, :]
            values += [jnp.where(masks[k], v, jnp.zeros_like(v)) for k in range(HIGH)]
        got = dot_nt(jnp.concatenate(values, axis=0), ones)
        half = 3 * HIGH * GROUP
        got = got[:half, :] + got[half:, :]
        for h in range(2):
            acc = jnp.zeros((GROUP, LANES), F32)
            for sa in range(3 * HIGH):
                piece = got[sa * GROUP : (sa + 1) * GROUP, h * LANES : (h + 1) * LANES]
                moved = jnp.concatenate(
                    [
                        pltpu.roll(piece[:8], sa, 1, stride=15, stride_axis=0),
                        pltpu.roll(piece[8:], sa + 8, 1, stride=15, stride_axis=0),
                    ],
                    axis=0,
                )
                acc = jnp.where(lane == sa, moved, acc)
            binned_ref[rows, h * LANES : (h + 1) * LANES] = acc
        return carry

    lax.fori_loop(0, blocks // GROUP, one_group, 0)

    capacity = 2 * blocks // patches
    patch_row = patch_ref[...].astype(F32)
    patch_col = jnp.broadcast_to(patch_row, (blocks, blocks)).T
    block_col = jnp.broadcast_to(block_ref[...].astype(F32), (blocks, blocks)).T
    earlier = iota((blocks, blocks), 0) < iota((blocks, blocks), 1)
    same = jnp.where((patch_col == patch_row) & earlier, 1.0, 0.0)
    position = patch_row * capacity + jnp.sum(same, axis=0, keepdims=True)
    select = (iota((2 * blocks, blocks), 0).astype(F32) == position).astype(F32).astype(BF16)
    turned = iota((blocks, LANES), 0)
    turned = turned + (turned >> 3 & 1)
    halves = []
    for h in range(2):
        part = binned_ref[:, h * LANES : (h + 1) * LANES]
        for bit in (1, 2, 4):
            part = jnp.where((turned & bit) != 0, pltpu.roll(part, LANES - 16 * bit, 1), part)
        halves.append(part)
    first = jnp.where(iota((blocks, LANES), 1) == LABEL_LANE, block_col + 1.0, halves[0])
    hi, lo = split2(jnp.concatenate([first, halves[1]], axis=1))
    payload = dot(jnp.concatenate([select, select], axis=1), jnp.concatenate([hi, lo], axis=0))
    out_ref[...] = jnp.where(iota(payload.shape, 1) == CURVE_LANE, curvature, payload)


def exchange(axis, count, me, send_at, recv_ref, send_sem, recv_sem):
    def one(step, carry):
        peer = lax.rem(me + step, count)
        pltpu.make_async_remote_copy(
            src_ref=send_at(peer),
            dst_ref=recv_ref.at[me],
            send_sem=send_sem,
            recv_sem=recv_sem,
            device_id={axis: peer},
            device_id_type=MESH,
        ).start()
        return carry

    lax.fori_loop(1, count, one, 0)
    pltpu.make_async_copy(send_at(me), recv_ref.at[me], recv_sem).start()
    pltpu.make_async_copy(recv_ref, recv_ref, recv_sem).wait()


def drain(count, recv_ref, send_sem):
    if count > 1:
        sent = recv_ref.at[pl.ds(0, count - 1)]
        pltpu.make_async_copy(sent, sent, send_sem).wait()


def link_kernel(
    patches, dets, pay_ref, res_ref, rz_ref, leg_ref, filt_ref, spread_ref, table_ref,
    new_ref, pre_ref, beta_ref,
    recv1, send2, recv2, send3, recv3, send4, recv4, send5, recv5, send_sems, recv_sems,
):
    my_patch, my_det = lax.axis_index("patch"), lax.axis_index("det")
    barrier = pltpu.get_barrier_semaphore()

    def greet(axis, count, me):
        def one(step, carry):
            pl.semaphore_signal(
                barrier, inc=1, device_id={axis: lax.rem(me + step, count)}, device_id_type=MESH
            )
            return carry

        lax.fori_loop(1, count, one, 0)

    greet("patch", patches, my_patch)
    greet("det", dets, my_det)
    pl.semaphore_wait(barrier, patches + dets - 2)

    capacity = recv1.shape[1]
    exchange(
        "patch", patches, my_patch, lambda p: pay_ref.at[p], recv1, send_sems.at[0], recv_sems.at[0]
    )
    got = recv1[...].reshape(patches * capacity, 256)
    hi, lo = split2(got)
    pick = (iota((16, LANES), 1) == LABEL_LANE).astype(F32).astype(BF16)
    labels = dot_nt(pick, hi[:, :LANES])[0:1, :]
    onehot = (iota((256, got.shape[0]), 0).astype(F32) + 1.0 == labels).astype(F32).astype(BF16)
    dense = dot(jnp.concatenate([onehot, onehot], axis=1), jnp.concatenate([hi, lo], axis=0))
    curve = jnp.sum(got, axis=0, keepdims=True) * (1.0 / capacity)
    dense = jnp.where(iota(dense.shape, 1) == CURVE_LANE, curve, dense)
    rows = 256 // dets
    send2[...] = dense.reshape(dets, rows, 256)
    exchange(
        "det", dets, my_det, lambda d: send2.at[d], recv2, send_sems.at[1], recv_sems.at[1]
    )
    image = jnp.sum(recv2[...], axis=0)
    rz_before = rz_ref[0]
    step_size = rz_before / image[0:1, CURVE_LANE : CURVE_LANE + 1]

    parts = split3(image)
    stacked = jnp.concatenate([p.astype(F32) for p in parts], axis=0).astype(BF16)
    wide = dot(stacked, spread_ref[...])
    wide = wide[:rows, :] + wide[rows : 2 * rows, :] + wide[2 * rows :, :]
    own_quarter = iota((rows, 256), 0) % 4 == iota((rows, 256), 1) // 64
    fields = []
    for s in range(3):
        old = res_ref[s]
        old = jnp.concatenate([old, old, old, old], axis=1)
        new = old - step_size * wide[:, s * 256 : (s + 1) * 256]
        new_ref[s] = new[:, :64]
        fields.append(jnp.where(own_quarter, new, 0.0))
    hi, lo = split2(jnp.concatenate(fields, axis=0))
    modes = dot(jnp.concatenate([hi, lo, hi], axis=1), table_ref[...])
    modes_here = LANES // dets
    slot = iota((dets, LANES), 1) // modes_here
    message = jnp.zeros((dets, LANES), F32)
    for ring in range(rows // 4):
        for s in range(3):
            at = s * rows + ring * 4
            line = jnp.sum(modes[at : at + 4, :], axis=0, keepdims=True)
            for e in range(2):
                target = ring * 16 + 2 * s + e
                wide_line = jnp.broadcast_to(line[:, e * LANES : (e + 1) * LANES], (dets, LANES))
                moved = pltpu.roll(wide_line, 0, 1, stride=modes_here, stride_axis=0)
                moved = pltpu.roll(moved, target * modes_here, 1)
                message = jnp.where(slot == target, moved, message)
    for d in range(dets):
        send3[d] = message[d : d + 1, :]
    exchange(
        "det", dets, my_det, lambda d: send3.at[d], recv3, send_sems.at[2], recv_sems.at[2]
    )

    cycles = recv3[...].reshape(dets, LANES)
    cycles = jnp.concatenate([cycles, pltpu.roll(cycles, 64, 1)], axis=0)
    cycles = jnp.concatenate([cycles, jnp.zeros((LANES - 2 * dets, LANES), F32)], axis=0).T
    columns = 6 * modes_here
    hi, lo = split2(cycles[: columns + 8, : 2 * dets])
    ring_of = iota((2 * dets, 2 * dets), 0)
    place = iota((2 * dets, 2 * dets), 1)
    order = (ring_of == 2 * (place % dets) + place // dets).astype(F32).astype(BF16)
    a, b, c = split3(leg_ref[...].reshape(modes_here * 64, 2 * dets))
    legendre = dot(a, order) + dot(b, order) + dot(c, order)
    leg_hi, leg_lo = split2(legendre)
    product = dot_nt(hi, leg_hi) + dot_nt(lo, leg_hi) + dot_nt(hi, leg_lo)
    mode_of = iota((columns, 64), 0) % modes_here
    coef = jnp.zeros((columns, 64), F32)
    for m in range(modes_here):
        coef = jnp.where(mode_of == m, product[:columns, m * 64 : (m + 1) * 64], coef)
    weight = jnp.concatenate([filt_ref[...]] * 6, axis=0)
    pre = weight * coef
    for c in range(6):
        pre_ref[c] = pre[c * modes_here : (c + 1) * modes_here, :]
    rz = jnp.sum(jnp.sum(pre * coef, axis=0, keepdims=True), axis=1, keepdims=True)
    send4[...] = jnp.broadcast_to(rz, (1, LANES))
    exchange("det", dets, my_det, lambda d: send4, recv4, send_sems.at[3], recv_sems.at[3])
    send5[...] = jnp.sum(recv4[...], axis=0)
    exchange("patch", patches, my_patch, lambda p: send5, recv5, send_sems.at[4], recv_sems.at[4])
    beta_ref[...] = jnp.sum(recv5[...], axis=0) / rz_before

    drain(patches, recv1, send_sems.at[0])
    drain(dets, recv2, send_sems.at[1])
    drain(dets, recv3, send_sems.at[2])
    drain(dets, recv4, send_sems.at[3])
    drain(patches, recv5, send_sems.at[4])


def per_device(
    patches, dets, tod_image, angles, pixel_offset, target_patch, target_block, noise_spectrum,
    residual, previous_rz, legendre, harmonic_filter,
):
    blocks, length = tod_image.shape[2:]
    vmem = pl.BlockSpec(memory_space=pltpu.VMEM)
    smem = pl.BlockSpec(memory_space=pltpu.SMEM)
    payload = pl.pallas_call(
        functools.partial(local_kernel, patches),
        out_shape=jax.ShapeDtypeStruct((2 * blocks, 256), F32),
        in_specs=[vmem] * 8,
        out_specs=vmem,
        scratch_shapes=[
            pltpu.VMEM((6, blocks, length), BF16),
            pltpu.VMEM((blocks, length), BF16),
            pltpu.VMEM((blocks, length), BF16),
            pltpu.VMEM((blocks, 256), F32),
        ],
        compiler_params=pltpu.CompilerParams(vmem_limit_bytes=40 * 1024 * 1024),
    )(
        tod_image[0, 0],
        angles[0, 0],
        pixel_offset[0, 0],
        target_patch.reshape(1, blocks),
        target_block.reshape(1, blocks),
        noise_spectrum[0, 0],
        jnp.asarray(fourier_matrix()),
        jnp.asarray(twiddle_rows()),
    )
    capacity = 2 * blocks // patches
    rows = residual.shape[1]
    modes_here = legendre.shape[0]
    new, pre, beta = pl.pallas_call(
        functools.partial(link_kernel, patches, dets),
        out_shape=(
            jax.ShapeDtypeStruct((3, rows, 64), F32),
            jax.ShapeDtypeStruct((6, modes_here, 64), F32),
            jax.ShapeDtypeStruct((1, LANES), F32),
        ),
        in_specs=[vmem, vmem, smem, vmem, vmem, vmem, vmem],
        out_specs=(vmem, vmem, vmem),
        scratch_shapes=[
            pltpu.VMEM((patches, capacity, 256), F32),
            pltpu.VMEM((dets, rows, 256), F32),
            pltpu.VMEM((dets, rows, 256), F32),
            pltpu.VMEM((dets, 1, LANES), F32),
            pltpu.VMEM((dets, 1, LANES), F32),
            pltpu.VMEM((1, LANES), F32),
            pltpu.VMEM((dets, 1, LANES), F32),
            pltpu.VMEM((1, LANES), F32),
            pltpu.VMEM((patches, 1, LANES), F32),
            pltpu.SemaphoreType.DMA((5,)),
            pltpu.SemaphoreType.DMA((5,)),
        ],
        compiler_params=pltpu.CompilerParams(
            collective_id=0, has_side_effects=True, vmem_limit_bytes=40 * 1024 * 1024
        ),
    )(
        payload.reshape(patches, capacity, 256),
        residual[0].transpose(1, 0, 2),
        previous_rz,
        legendre,
        harmonic_filter,
        jnp.asarray(pixel_spread()),
        jnp.asarray(cycle_matrix(modes_here)),
    )
    return new.transpose(1, 0, 2)[None], pre.transpose(1, 0, 2)[None], beta[0, :1]


def solution(mesh):
    placed = (
        P("patch", "det", None, None),
        P("patch", "det", None, None),
        P("patch", "det", None, None),
        P("patch", "det", None, None),
        P("patch", "det", None),
        P("patch", "det", None, None),
        P("patch", "det", None, None),
        P(),
        P("det", None, None),
        P("det", None),
    )
    return jax.shard_map(
        functools.partial(per_device, mesh.shape["patch"], mesh.shape["det"]),
        mesh=mesh,
        in_specs=placed,
        out_specs=(P("patch", "det", None, None), P("patch", "det", None, None), P()),
        check_vma=False,
    )
```

time: 517 us -> 83.4 us (0.16); the launches traced: 507 us -> 83 us
  blocking collectives: 329 us -> 0 us
  matrix products: 77.4 us -> 0 us
  Pallas kernels: 0 us -> 74.5 us
  starting transfers between devices: 33.5 us -> 0 us
  waiting for transfers between devices: 32.1 us -> 0 us
  between operations: 17.6 us -> 2.57 us
  local copies, waits for them, and re-layouts: 12.3 us -> 6.01 us
  other arithmetic: 5.29 us -> 0 us
    psum x2 -> x0, blocking collectives: 268 us -> none  [the longest x1 152 us: per_device(): lax.psum(jnp.sum(preconditioned * coefficients), ('patch', 'det'))]
    dot_general x18 -> x0, matrix products: 77.4 us -> none  [the longest x8 16.1 us: one_group(): return jnp.einsum('gst,gtk->gsk', values, onehot, precision=PRECISE)]
    pallas_call x0 -> x2, Pallas kernels: none -> 74.5 us  [the longest x1 67.7 us: per_device(): pl.pallas_call(functools.partial(link_kernel, patches, dets), out_shape=(...]
    all_gather x1 -> x0, blocking collectives: 60.8 us -> none  [cycle_coefficients(): cycle_piece = lax.all_gather(along_cycle, 'det', axis=1, tiled=True)]
    all_to_all x2 -> x0, starting transfers between devices: 33.5 us -> none  [the longest x1 21.3 us: per_device(): lax.all_to_all(labels.reshape(patches, capacity), 'patch', split_axis=0,...]
    reduce_scatter x1 -> x0, waiting for transfers between devices: 18.1 us -> none  [per_device(): lax.psum_scatter(jnp.dot(onehot, flat_payload, precision=PRECISE), 'det',...]
    all_to_all x2 -> x0, waiting for transfers between devices: 14 us -> none  [the longest x1 14 us: per_device(): lax.all_to_all(payload.reshape(patches, capacity, 3 * pixel_count), 'patc...]
    eq x9 -> x0, local copies, waits for them, and re-layouts: 6.95 us -> none  [the longest x8 6.86 us: one_group(): onehot = (places[:, :, None] == pixel_index).astype(jnp.float32)]
  transfers between devices with their start and end apart: 3 -> 0, of which waited for: 2 -> 0; matrix products, arithmetic and copies ran while one was open for 17% -> 0% of each run, Pallas kernels for 0% -> 0%
where the time goes in v1:
time: 83.4 us; the launch traced here: 83 us
  Pallas kernels  74.5 us (89%)
  local copies, waits for them, and re-layouts  6.01 us (7%)
  between operations  2.57 us (3%)
    pallas_call x1, Pallas kernels, per_device(): pl.pallas_call(functools.partial(link_kernel, patches, dets), out_shape=(...  67.7 us
    pallas_call x1, Pallas kernels, per_device(): pl.pallas_call(functools.partial(local_kernel, patches), out_shape=jax.Sh...  6.81 us
    unnamed x28, local copies, waits for them, and re-layouts  6.01 us

profile of v1, /device:TPU:1, one launch (start us, length us, event | category | flops | bytes accessed | tf_op | source)
XLA Modules:
  0.0 83.0 jit_solution(17816187840338646314)
XLA Ops:
  0.6 0.0 copy-start.8
  1.3 0.0 copy-start.9
  1.3 0.0 copy-start.11
  1.3 0.0 copy-start.12
  1.3 0.0 copy-done.8
  1.3 0.6 copy-done.9
  2.0 0.0 copy-done.11
  2.0 0.0 copy-done.12
  2.0 0.0 copy-start
  2.0 1.0 %copy-done = f32[1,1,128,1024]{3,2,1,0:T(8,128)S(1)} copy-done((f32[1,1,128,1024]{3,2,1,0:T(8,128)S(1)}, f32[1,1,128,1024]{3,2,1,0:T(8,128)}, u32[]{:S(2)}) %copy-start) | copy-done | bytes 524312
  3.0 0.0 copy-start.1
  3.0 1.0 %copy-done.1 = f32[1,1,128,1024]{3,2,1,0:T(8,128)S(1)} copy-done((f32[1,1,128,1024]{3,2,1,0:T(8,128)S(1)}, f32[1,1,128,1024]{3,2,1,0:T(8,128)}, u32[]{:S(2)}) %copy-start.1) | copy-done | bytes 524312
  4.1 0.0 copy-start.2
  4.1 1.0 %copy-done.2 = s32[1,1,128,1024]{3,2,1,0:T(8,128)S(1)} copy-done((s32[1,1,128,1024]{3,2,1,0:T(8,128)S(1)}, s32[1,1,128,1024]{3,2,1,0:T(8,128)}, u32[]{:S(2)}) %copy-start.2) | copy-done | bytes 524312
  5.1 0.0 copy-start.3
  5.1 1.0 %copy-done.3 = bf16[768,256]{1,0:T(8,128)(2,1)S(1)} copy-done((bf16[768,256]{1,0:T(8,128)(2,1)S(1)}, bf16[768,256]{1,0:T(8,128)(2,1)}, u32[]{:S(2)}) %copy-start.3) | copy-done | bytes 393240
  6.1 0.0 copy-start.4
  6.1 0.0 copy-start.5
  6.1 0.0 copy-start.6
  6.1 0.0 copy-start.7
  6.1 0.0 copy-start.10
  6.1 6.8 %shard_map.157 = f32[256,256]{1,0:T(8,128)S(1)} custom-call(f32[128,1024]{1,0:T(8,128)S(1)} %bitcast.19, f32[128,1024]{1,0:T(8,128)S(1)} %bitcast.20, s32[128,1024]{1,0:T(8,128)S(1)} %bitcast.21, s32[1,128]{1,0:T(1,128)S(1)} %bitcast.26, s32[1,128]{1,0:T(1,128)S(1)} %bitcast.27, f32[4,513]{1,0:T(4,128)S(1)} %bitcast.25, bf16[768,256]{1,0:T(8,128)(2,1)S(1)} %copy-done.3, ...), custom_call_target="tpu_custom_call" | custom-call | tf_op jit(solution)/shard_map/pallas_call | solution.py:398
  13.0 0.0 copy-done.4
  13.0 0.0 copy-done.5
  13.0 0.0 copy-done.6
  13.0 0.0 copy-done.7
  13.0 0.0 copy-done.10
  13.0 67.7 %shard_map.158 = (f32[3,8,64]{2,1,0:T(8,128)S(1)}, f32[6,4,64]{2,1,0:T(4,128)S(1)}, f32[1,128]{1,0:T(1,128)S(1)}) custom-call(f32[32,8,256]{2,1,0:T(8,128)S(1)} %bitcast.18, f32[3,8,64]{2,1,0:T(8,128)S(1)} %bitcast.22, f32[1]{0:T(128)S(6)} %copy.20.rz_ref, f32[4,64,64]{2,1,0:T(8,128)S(1)} %copy-done.6, f32[4,64]{1,0:T(4,128)S(1)} %copy-done.10, ...), custom_call_target="tpu_custom_call" | custom-call | tf_op jit(solution)/shard_map/pallas_call | solution.py:423
  80.7 0.6 copy.21
  81.3 0.6 copy.22
Async XLA Ops:
  0.6 0.7 copy-start.8
  1.3 0.7 copy-start.9
  1.3 0.7 copy-start.11
  1.3 0.7 copy-start.12
  2.0 1.0 %copy-start = (f32[1,1,128,1024]{3,2,1,0:T(8,128)S(1)}, f32[1,1,128,1024]{3,2,1,0:T(8,128)}, u32[]{:S(2)}) copy-start(f32[1,1,128,1024]{3,2,1,0:T(8,128)} %param.14) | copy-start | bytes 1572868
  3.0 1.0 %copy-start.1 = (f32[1,1,128,1024]{3,2,1,0:T(8,128)S(1)}, f32[1,1,128,1024]{3,2,1,0:T(8,128)}, u32[]{:S(2)}) copy-start(f32[1,1,128,1024]{3,2,1,0:T(8,128)} %param.15) | copy-start | bytes 1572868
  4.1 1.0 %copy-start.2 = (s32[1,1,128,1024]{3,2,1,0:T(8,128)S(1)}, s32[1,1,128,1024]{3,2,1,0:T(8,128)}, u32[]{:S(2)}) copy-start(s32[1,1,128,1024]{3,2,1,0:T(8,128)} %param.16) | copy-start | bytes 1572868
  5.1 1.0 %copy-start.3 = (bf16[768,256]{1,0:T(8,128)(2,1)S(1)}, bf16[768,256]{1,0:T(8,128)(2,1)}, u32[]{:S(2)}) copy-start(bf16[768,256]{1,0:T(8,128)(2,1)} %constant.8.clone.table_ref) | copy-start | bytes 1179652
  6.1 6.8 %copy-start.4 = (bf16[768,256]{1,0:T(8,128)(2,1)S(1)}, bf16[768,256]{1,0:T(8,128)(2,1)}, u32[]{:S(2)}) copy-start(bf16[768,256]{1,0:T(8,128)(2,1)} %constant.11.clone.table_ref) | copy-start | bytes 1179652
  6.1 6.8 %copy-start.5 = (bf16[256,768]{1,0:T(8,128)(2,1)S(1)}, bf16[256,768]{1,0:T(8,128)(2,1)}, u32[]{:S(2)}) copy-start(bf16[256,768]{1,0:T(8,128)(2,1)} %constant.10.clone.spread_ref) | copy-start | bytes 1179652
  6.1 6.9 %copy-start.6 = (f32[4,64,64]{2,1,0:T(8,128)S(1)}, f32[4,64,64]{2,1,0:T(8,128)}, u32[]{:S(2)}) copy-start(f32[4,64,64]{2,1,0:T(8,128)} %leg_ref.1) | copy-start | bytes 196612
  6.1 6.9 %copy-start.7 = (f32[1,8,3,64]{3,1,2,0:T(8,128)S(1)}, f32[1,8,3,64]{3,1,2,0:T(8,128)}, u32[]{:S(2)}) copy-start(f32[1,8,3,64]{3,1,2,0:T(8,128)} %param.20) | copy-start | bytes 18436
  6.1 6.9 %copy-start.10 = (f32[4,64]{1,0:T(4,128)S(1)}, f32[4,64]{1,0:T(4,128)}, u32[]{:S(2)}) copy-start(f32[4,64]{1,0:T(4,128)} %filt_ref.1) | copy-start | bytes 3076

commit v2 on v1

v2 whole, which is shorter than its diff:
```python
import functools
import math

import jax
import jax.numpy as jnp
import numpy as np
from jax import lax
from jax.experimental import pallas as pl
from jax.experimental.pallas import tpu as pltpu
from jax.sharding import PartitionSpec as P

BF16 = jnp.bfloat16
F32 = jnp.float32
I32 = jnp.int32
MESH = pl.DeviceIdType.MESH
LANES = 128
RADIX = 8
GROUP = 16
HIGH = 4
LOW = 16
ROOT_HALF = math.sqrt(0.5)


def split2(x):
    hi = x.astype(BF16)
    return hi, (x - hi.astype(F32)).astype(BF16)


def split3(x):
    hi = x.astype(BF16)
    rest = x - hi.astype(F32)
    mid = rest.astype(BF16)
    return hi, mid, (rest - mid.astype(F32)).astype(BF16)


def dot(a, b):
    return lax.dot_general(a, b, (((1,), (0,)), ((), ())), preferred_element_type=F32)


def dot_nt(a, b):
    return lax.dot_general(a, b, (((1,), (1,)), ((), ())), preferred_element_type=F32)


def iota(shape, dim):
    return lax.broadcasted_iota(I32, shape, dim)


def stack_table(table):
    hi, lo = split2(table)
    return jnp.concatenate([hi, hi, lo], axis=0)


def fourier_matrix():
    j = np.arange(LANES)
    angle = 2.0 * np.pi * (np.outer(j, j) % LANES) / LANES
    c, s = np.cos(angle), np.sin(angle)
    return np.block([[c, -s], [s, c]]).astype(np.float32)


def twiddle_rows():
    n = np.arange(LANES)
    angle = [2.0 * np.pi * n * k / (RADIX * LANES) for k in range(1, 5)]
    return np.stack([np.cos(a) for a in angle] + [np.sin(a) for a in angle]).astype(np.float32)


def cycle_matrix(modes_here):
    f = np.arange(256)[:, None]
    lane = np.arange(LANES)
    mode = (-(lane // modes_here) % (LANES // modes_here)) * modes_here + lane % modes_here
    angle = 2.0 * np.pi * (f * mode % 256) / 256.0
    scale = math.sqrt(2.0 / 256.0)
    return (np.concatenate([np.cos(angle), np.sin(angle)], axis=1) * scale).astype(np.float32)


def mode_rows(modes_here):
    row = np.arange(256)[:, None]
    owner, e, m = row // (2 * modes_here), row // modes_here % 2, row % modes_here
    mode = owner * modes_here + m
    angle = 2.0 * np.pi * (np.arange(256) * mode % 256) / 256.0
    rows = np.where(e == 0, np.cos(angle), np.sin(angle)) * math.sqrt(2.0 / 256.0)
    return rows.astype(np.float32)


def pixel_order():
    col = iota((1, 256), 1)
    s, pixel = col // 64, col % 64
    a, c = pixel // LOW, pixel % LOW
    source = jnp.where(s < 3, (c // 8) * LANES + (c % 8) * 16 + s * HIGH + a, -1)
    return (iota((256, 256), 0) == source).astype(F32).astype(BF16)


def double_angle(theta):
    n = jnp.round(theta * (2.0 / math.pi))
    odd = (n.astype(I32) & 1) == 1
    hi = np.float32(math.pi / 2)
    lo = np.float32(math.pi / 2 - float(hi))
    r = (theta - n * hi) - n * lo
    y = r * r
    c = jnp.full_like(y, COS_POLY[-1])
    for coef in COS_POLY[-2::-1]:
        c = c * y + coef
    s = jnp.full_like(y, SIN_POLY[-1])
    for coef in SIN_POLY[-2::-1]:
        s = s * y + coef
    return odd, c, s * r


def fit_polys():
    top = (math.pi / 4) ** 2 * 1.0001
    y = top * 0.5 * (1.0 - np.cos(np.pi * (np.arange(400) + 0.5) / 400))
    r = np.sqrt(y)
    power = y[:, None] ** np.arange(6)
    cos_c = np.linalg.lstsq(power, np.cos(2 * r), rcond=None)[0]
    sin_c = np.linalg.lstsq(power[:, :5], np.sin(2 * r) / r, rcond=None)[0]
    return [float(np.float32(v)) for v in cos_c], [float(np.float32(v)) for v in sin_c]


COS_POLY, SIN_POLY = fit_polys()


def filter_blocks(x, spec_ref, table, tw):
    blocks = x.shape[0]
    dets = spec_ref.shape[0]
    t = [x[:, i * LANES : (i + 1) * LANES] for i in range(RADIX)]
    a = [t[i] + t[i + 4] for i in range(4)]
    b = [t[i] - t[i + 4] for i in range(4)]
    even, odd = a[0] + a[2], a[1] + a[3]
    diff, both = (b[1] - b[3]) * ROOT_HALF, (b[1] + b[3]) * ROOT_HALF
    y = [
        (even + odd, None),
        (b[0] + diff, -(b[2] + both)),
        (a[0] - a[2], a[3] - a[1]),
        (b[0] - diff, b[2] - both),
        (even - odd, None),
    ]
    rows = [jnp.concatenate([y[0][0], jnp.zeros_like(x[:, :LANES])], axis=1)]
    for k in range(1, 5):
        c, s = tw[k - 1 : k, :], tw[k + 3 : k + 4, :]
        re, im = y[k]
        if im is None:
            rows.append(jnp.concatenate([re * c, -(re * s)], axis=1))
        else:
            rows.append(jnp.concatenate([re * c + im * s, im * c - re * s], axis=1))
    hi, lo = split2(jnp.concatenate(rows, axis=0))
    spectrum = dot(jnp.concatenate([hi, lo, hi], axis=1), table)

    col = iota((1, 5 * LANES), 1)
    k_of, j_of = col // LANES, col % LANES
    order = k_of + RADIX * j_of
    place = jnp.minimum(order, RADIX * LANES - order)
    pick = (iota((512, 5 * LANES), 0) == place).astype(F32).astype(BF16)
    own = spec_ref[...]
    parts = split3(own[:, :512])
    weight = dot(parts[0], pick) + dot(parts[1], pick) + dot(parts[2], pick)
    weight = weight + jnp.where(place == 512, own[:, 512:513], 0.0)
    edge = (k_of == 0) | (k_of == 4)
    weight = weight * jnp.where(edge, 1.0 / 1024.0, 2.0 / 1024.0)

    per = blocks // dets
    scaled = []
    for k in range(5):
        w = weight[:, k * LANES : (k + 1) * LANES]
        w = jnp.concatenate([w, -w], axis=1)
        for d in range(dets):
            part = spectrum[k * blocks + d * per : k * blocks + (d + 1) * per, :]
            scaled.append(part * w[d : d + 1, :])
    hi, lo = split2(jnp.concatenate(scaled, axis=0))
    u = dot(jnp.concatenate([hi, lo, hi], axis=1), table)
    re = [u[k * blocks : (k + 1) * blocks, :LANES] for k in range(5)]
    im = [u[k * blocks : (k + 1) * blocks, LANES:] for k in range(5)]
    tr, ti = [re[0]], [None]
    for k in range(1, 5):
        c, s = tw[k - 1 : k, :], tw[k + 3 : k + 4, :]
        tr.append(re[k] * c + im[k] * s)
        ti.append(re[k] * s - im[k] * c)
    plus, minus = tr[0] + tr[4], tr[0] - tr[4]
    p1, m1 = (tr[1] + ti[1]) * ROOT_HALF, (tr[1] - ti[1]) * ROOT_HALF
    p3, m3 = (tr[3] + ti[3]) * ROOT_HALF, (tr[3] - ti[3]) * ROOT_HALF
    e0, e1 = plus + tr[2], tr[1] + tr[3]
    f0, f1 = plus - tr[2], ti[3] - ti[1]
    g0, g1 = minus - ti[2], m1 - p3
    h0, h1 = minus + ti[2], m3 - p1
    return [e0 + e1, g0 + g1, f0 + f1, h0 + h1, e0 - e1, g0 - g1, f0 - f1, h0 - h1]


def bin_blocks(filtered, angle_ref, offset_ref, val_ref, low_ref, high_ref, binned_ref):
    blocks = angle_ref.shape[0]
    for i in range(RADIX):
        at = slice(i * LANES, (i + 1) * LANES)
        f = filtered[i]
        odd, c, s = double_angle(angle_ref[:, at])
        turned = jnp.where(odd, -f, f)
        for comp, v in enumerate((f, turned * c, turned * s)):
            hi, lo = split2(v)
            val_ref[comp, :, at] = hi
            val_ref[3 + comp, :, at] = lo
        off = offset_ref[:, at]
        low_ref[:, at] = (off & (LOW - 1)).astype(F32).astype(BF16)
        high_ref[:, at] = (off >> 4).astype(F32).astype(BF16)
    lane = iota((GROUP, LANES), 1) % 16

    def one_group(g, carry):
        rows = pl.ds(pl.multiple_of(g * GROUP, GROUP), GROUP)
        low, high = low_ref[rows, :], high_ref[rows, :]
        ones = jnp.concatenate(
            [jnp.where(low == k, 1.0, 0.0).astype(BF16) for k in range(LOW)], axis=0
        )
        masks = [high == k for k in range(HIGH)]
        values = []
        for comp in range(6):
            v = val_ref[comp, rows, :]
            values += [jnp.where(masks[k], v, jnp.zeros_like(v)) for k in range(HIGH)]
        got = dot_nt(jnp.concatenate(values, axis=0), ones)
        half = 3 * HIGH * GROUP
        got = got[:half, :] + got[half:, :]
        for h in range(2):
            acc = jnp.zeros((GROUP, LANES), F32)
            for sa in range(3 * HIGH):
                piece = got[sa * GROUP : (sa + 1) * GROUP, h * LANES : (h + 1) * LANES]
                moved = jnp.concatenate(
                    [
                        pltpu.roll(piece[:8], sa, 1, stride=15, stride_axis=0),
                        pltpu.roll(piece[8:], sa + 8, 1, stride=15, stride_axis=0),
                    ],
                    axis=0,
                )
                acc = jnp.where(lane == sa, moved, acc)
            binned_ref[rows, h * LANES : (h + 1) * LANES] = acc
        return carry

    lax.fori_loop(0, blocks // GROUP, one_group, 0)
    turned = iota((blocks, LANES), 0)
    turned = turned + (turned >> 3 & 1)
    halves = []
    for h in range(2):
        part = binned_ref[:, h * LANES : (h + 1) * LANES]
        for bit in (1, 2, 4):
            part = jnp.where((turned & bit) != 0, pltpu.roll(part, LANES - 16 * bit, 1), part)
        halves.append(part)
    return jnp.concatenate(halves, axis=1)


def route(patches, binned, curvature, patch_row, block_row, order):
    blocks = binned.shape[0]
    capacity = 2 * blocks // patches
    quarter = capacity // 2
    hi, lo = split2(binned)
    moved = dot(jnp.concatenate([hi, lo], axis=1), jnp.concatenate([order, order], axis=0))
    patch_row = patch_row.astype(F32)
    block_row = block_row.astype(F32)
    patch_col = jnp.broadcast_to(patch_row, (blocks, blocks)).T
    same = patch_col == patch_row
    above = iota((blocks, blocks), 0)
    beside = iota((blocks, blocks), 1)
    slot_row = jnp.sum(jnp.where(same & (above < beside), 1.0, 0.0), axis=0, keepdims=True)
    slot_col = jnp.sum(jnp.where(same & (beside < above), 1.0, 0.0), axis=1, keepdims=True)
    place = patch_row * capacity + slot_row
    row = iota((2 * blocks, blocks), 0)
    own = row.astype(F32)
    first_half = row % capacity < quarter

    def choose(hit):
        return hit.astype(F32).astype(BF16)

    select = choose(own == place)
    select_a = choose((own == place) & first_half)
    select_b = choose((own + quarter == place) & first_half)
    hi, lo = split2(moved[:, :LANES])
    front = dot(jnp.concatenate([select, select], axis=1), jnp.concatenate([hi, lo], axis=0))
    back = moved[:, LANES:]
    hi, lo = split2(back)
    hi2, lo2 = split2(pltpu.roll(back, 64, 1))
    back = dot(
        jnp.concatenate([select_a, select_a, select_b, select_b], axis=1),
        jnp.concatenate([hi, lo, hi2, lo2], axis=0),
    )
    named = jnp.where((row // capacity).astype(F32) == patch_row, block_row + 1.0, 0.0)
    slot_lane = (iota((blocks, LANES), 1) % capacity).astype(F32)
    labels = dot(named.astype(BF16), choose(slot_col == slot_lane))
    labels = jnp.where(iota(labels.shape, 1) < 64, labels, curvature)
    back = jnp.where(iota(back.shape, 0) % capacity == quarter, labels, back)
    return front, back


def start_exchange(axis, count, me, send_at, recv_at, send_sem, recv_sem):
    def one(step, carry):
        peer = lax.rem(me + step, count)
        pltpu.make_async_remote_copy(
            src_ref=send_at(peer),
            dst_ref=recv_at(me),
            send_sem=send_sem,
            recv_sem=recv_sem,
            device_id={axis: peer},
            device_id_type=MESH,
        ).start()
        return carry

    lax.fori_loop(1, count, one, 0)
    pltpu.make_async_copy(send_at(me), recv_at(me), recv_sem).start()


def await_bytes(ref, sem):
    pltpu.make_async_copy(ref, ref, sem).wait()


def fold_rows(x, step):
    wrapped = pltpu.roll(pltpu.roll(x, x.shape[0] - step, 0), 64, 1)
    return jnp.where(iota(x.shape, 1) < 64, x, wrapped)


def legendre_columns(columns, legendre, modes_here):
    hi, lo = split2(columns)
    leg_hi, leg_lo = split2(legendre)
    product = dot_nt(hi, leg_hi) + dot_nt(lo, leg_hi) + dot_nt(hi, leg_lo)
    rows = 6 * modes_here
    mode_of = iota((rows, 64), 0) % modes_here
    coef = jnp.zeros((rows, 64), F32)
    for m in range(modes_here):
        coef = jnp.where(mode_of == m, product[:rows, m * 64 : (m + 1) * 64], coef)
    return coef


def step_kernel(patches, dets, *refs):
    hbm, refs = refs[:INPUTS], refs[INPUTS:]
    (new_ref, pre_ref, beta_ref), refs = refs[:3], refs[3:]
    held, refs = refs[:INPUTS], refs[INPUTS:]
    (
        val_ref, low_ref, high_ref, binned_ref,
        send1, recv1, send2, recv2, send3, recv3, send_map, recv_map, send4, recv4, send5, recv5,
        in_sems, send_sems, recv_sems,
    ) = refs
    my_patch, my_det = lax.axis_index("patch"), lax.axis_index("det")
    fetches = [
        pltpu.make_async_copy(src, dst, in_sems.at[i]) for i, (src, dst) in enumerate(zip(hbm, held))
    ]
    for fetch in fetches:
        fetch.start()
    barrier = pltpu.get_barrier_semaphore()

    def greet(axis, count, me):
        def one(step, carry):
            pl.semaphore_signal(
                barrier, inc=1, device_id={axis: lax.rem(me + step, count)}, device_id_type=MESH
            )
            return carry

        lax.fori_loop(1, count, one, 0)

    greet("patch", patches, my_patch)
    greet("det", dets, my_det)
    (
        x_ref, table_ref, tw_ref, spec_ref, angle_ref, offset_ref, patch_ref, block_ref,
        res_ref, cycle_ref, modes_ref, leg_ref, filt_ref, rz_ref,
    ) = held

    for fetch in fetches[:4]:
        fetch.wait()
    x = x_ref[...]
    filtered = filter_blocks(x, spec_ref, stack_table(table_ref[...]), tw_ref[...])
    total = jnp.zeros((x.shape[0], LANES), F32)
    for i in range(RADIX):
        total = total + x[:, i * LANES : (i + 1) * LANES] * filtered[i]
    curvature = jnp.sum(jnp.sum(total, axis=0, keepdims=True), axis=1, keepdims=True)
    for fetch in fetches[4:]:
        fetch.wait()
    binned = bin_blocks(filtered, angle_ref, offset_ref, val_ref, low_ref, high_ref, binned_ref)
    front, back = route(
        patches, binned, curvature, patch_ref[...], block_ref[...], pixel_order()
    )
    capacity = front.shape[0] // patches
    half = capacity // 2
    send1[:, :capacity, :] = front.reshape(patches, capacity, LANES)
    send1[:, capacity:, :] = back.reshape(patches, capacity, LANES)
    pl.semaphore_wait(barrier, patches + dets - 2)
    used1 = capacity + half + 1
    start_exchange(
        "patch", patches, my_patch,
        lambda p: send1.at[p, pl.ds(0, used1)], lambda p: recv1.at[p, pl.ds(0, used1)],
        send_sems.at[0], recv_sems.at[0],
    )

    rows = res_ref.shape[1]
    modes_here = LANES // dets
    lines = []
    for s in range(3):
        old = res_ref[s]
        for ring in range(rows // 4):
            lines.append(
                jnp.concatenate([old[ring * 4 + q : ring * 4 + q + 1, :] for q in range(4)], axis=1)
            )
    lines.append(jnp.zeros((8 - len(lines), 256), F32))
    hi, lo = split2(jnp.concatenate(lines, axis=0))
    modes = dot(jnp.concatenate([hi, lo, hi], axis=1), stack_table(cycle_ref[...]))
    slot = iota((dets, LANES), 1) // modes_here
    message = jnp.zeros((dets, LANES), F32)
    for s in range(3):
        for ring in range(rows // 4):
            at = s * (rows // 4) + ring
            for e in range(2):
                target = ring * 16 + 2 * s + e
                line = modes[at : at + 1, e * LANES : (e + 1) * LANES]
                moved = pltpu.roll(
                    jnp.broadcast_to(line, (dets, LANES)), 0, 1, stride=modes_here, stride_axis=0
                )
                moved = pltpu.roll(moved, target * modes_here, 1)
                message = jnp.where(slot == target, moved, message)
    for d in range(dets):
        send3[d] = message[d : d + 1, :]
    start_exchange(
        "det", dets, my_det, lambda d: send3.at[d], lambda d: recv3.at[d],
        send_sems.at[2], recv_sems.at[2],
    )

    await_bytes(recv1.at[:, pl.ds(0, used1)], recv_sems.at[0])
    got0 = recv1[:, :capacity, :].reshape(patches * capacity, LANES)
    got1 = recv1[:, capacity:, :]
    tags = jnp.sum(jnp.where(iota(got1.shape, 1) == half, got1, 0.0), axis=1)
    got1 = jnp.where(iota(got1.shape, 1) < half, got1, 0.0).reshape(patches * capacity, LANES)
    curve = jnp.sum(tags, axis=0, keepdims=True)
    tags = jnp.where(iota(tags.shape, 1) < 64, tags, pltpu.roll(tags, 64, 1))
    per = LANES // capacity
    labels = jnp.concatenate(
        [
            jnp.sum(
                jnp.where(iota(tags.shape, 1) // capacity + h * per == iota(tags.shape, 0), tags, 0.0),
                axis=0,
                keepdims=True,
            )
            for h in range(patches // per)
        ],
        axis=1,
    )
    labels_b = pltpu.roll(labels, labels.shape[1] - half, 1)
    hi, lo = split2(got0)
    rhs0 = jnp.concatenate([hi, lo], axis=0)
    hi, lo = split2(got1)
    hi2, lo2 = split2(pltpu.roll(got1, 64, 1))
    rhs1 = jnp.concatenate([hi, lo, hi2, lo2], axis=0)

    def spread(target):
        hit = (target == labels).astype(F32).astype(BF16)
        hit_b = (target == labels_b).astype(F32).astype(BF16)
        return (
            dot(jnp.concatenate([hit, hit], axis=1), rhs0),
            dot(jnp.concatenate([hit, hit, hit_b, hit_b], axis=1), rhs1),
        )

    row = iota((256, patches * capacity), 0)
    map0, map1 = spread((row % 64 * 4 + row // 64 + 1).astype(F32))
    left = iota((64, LANES), 1) < 64
    fields = []
    for s in range(3):
        source = map1 if s == 2 else map0
        tiles = []
        for h in range(2):
            a = source[h * 128 : h * 128 + 64, :]
            b = source[h * 128 + 64 : h * 128 + 128, :]
            if s == 1:
                tiles.append(jnp.where(left, pltpu.roll(a, 64, 1), b))
            else:
                tiles.append(jnp.where(left, a, pltpu.roll(b, 64, 1)))
        fields.append(jnp.concatenate(tiles, axis=1))
    hi, lo = split2(jnp.concatenate(fields, axis=0))
    mode_hi, mode_lo = split2(modes_ref[...])
    modes = dot_nt(
        jnp.concatenate([mode_hi, mode_lo, mode_hi], axis=1),
        jnp.concatenate([hi, hi, lo], axis=1),
    )
    group = 2 * modes_here
    modes1 = fold_rows(
        jnp.concatenate([modes[:, LANES:], jnp.zeros((256, 64), F32)], axis=1), modes_here
    )
    modes1 = jnp.where(iota(modes1.shape, 0) % group == modes_here, curve, modes1)
    send2[:, :group, :] = modes[:, :LANES].reshape(dets, group, LANES)
    send2[:, group:, :] = modes1.reshape(dets, group, LANES)
    used2 = group + modes_here + 1
    start_exchange(
        "det", dets, my_det,
        lambda d: send2.at[d, pl.ds(0, used2)], lambda d: recv2.at[d, pl.ds(0, used2)],
        send_sems.at[1], recv_sems.at[1],
    )

    map0, map1 = spread((row + 1).astype(F32))
    used_map = rows + rows // 2
    send_map[:, :rows, :] = map0.reshape(dets, rows, LANES)
    send_map[:, rows:, :] = fold_rows(map1, rows // 2).reshape(dets, rows, LANES)
    start_exchange(
        "det", dets, my_det,
        lambda d: send_map.at[d, pl.ds(0, used_map)], lambda d: recv_map.at[d, pl.ds(0, used_map)],
        send_sems.at[5], recv_sems.at[5],
    )

    await_bytes(recv3, recv_sems.at[2])
    cycles = recv3[...].reshape(dets, LANES)
    cycles = jnp.concatenate([cycles, pltpu.roll(cycles, 64, 1)], axis=0)
    cycles = jnp.concatenate([cycles, jnp.zeros((LANES - 2 * dets, LANES), F32)], axis=0).T
    columns = 6 * modes_here
    ring_of = iota((2 * dets, 2 * dets), 0)
    place = iota((2 * dets, 2 * dets), 1)
    order = (ring_of == 2 * (place % dets) + place // dets).astype(F32).astype(BF16)
    legendre = leg_ref[...].reshape(modes_here * 64, 2 * dets)
    a, b, c = split3(legendre)
    coef_old = legendre_columns(
        cycles[: columns + 8, : 2 * dets], dot(a, order) + dot(b, order) + dot(c, order), modes_here
    )
    weight = jnp.concatenate([filt_ref[...]] * 6, axis=0)
    rz_before = rz_ref[...]

    await_bytes(recv2.at[:, pl.ds(0, used2)], recv_sems.at[1])
    sum0 = jnp.sum(recv2[:, :group, :], axis=0)
    sum1 = jnp.sum(recv2[:, group:, :], axis=0)
    step_size = rz_before / sum1[modes_here : modes_here + 1, 64:65]
    turned0, turned1 = pltpu.roll(sum0, 64, 1), pltpu.roll(sum1, 64, 1)
    image_modes = jnp.concatenate(
        [sum0, turned0, sum1[:modes_here], turned1[:modes_here], jnp.zeros((8, LANES), F32)], axis=0
    )[:, :64]
    coef = coef_old - step_size * legendre_columns(image_modes, legendre, modes_here)
    pre = weight * coef
    rz = jnp.sum(jnp.sum(pre * coef, axis=0, keepdims=True), axis=1, keepdims=True)
    send4[...] = jnp.broadcast_to(rz, (1, LANES))
    start_exchange(
        "det", dets, my_det, lambda d: send4, lambda d: recv4.at[d], send_sems.at[3], recv_sems.at[3]
    )
    for c in range(6):
        pre_ref[c] = pre[c * modes_here : (c + 1) * modes_here, :]
    await_bytes(recv_map.at[:, pl.ds(0, used_map)], recv_sems.at[5])
    image0 = jnp.sum(recv_map[:, :rows, :], axis=0)
    image1 = jnp.sum(recv_map[:, rows:, :], axis=0)
    low = rows // 2
    image1 = jnp.concatenate([image1[:low], pltpu.roll(image1, 64, 1)[:low]], axis=0)
    new_ref[0] = res_ref[0] - step_size * image0[:, :64]
    new_ref[1] = res_ref[1] - step_size * pltpu.roll(image0, 64, 1)[:, :64]
    new_ref[2] = res_ref[2] - step_size * image1[:, :64]

    await_bytes(recv4, recv_sems.at[3])
    send5[...] = jnp.sum(recv4[...], axis=0)
    start_exchange(
        "patch", patches, my_patch, lambda p: send5, lambda p: recv5.at[p],
        send_sems.at[4], recv_sems.at[4],
    )
    await_bytes(recv5, recv_sems.at[4])
    beta_ref[...] = jnp.sum(recv5[...], axis=0) / rz_before

    others = pl.ds(0, patches - 1)
    await_bytes(recv1.at[others, pl.ds(0, used1)], send_sems.at[0])
    await_bytes(recv5.at[others], send_sems.at[4])
    others = pl.ds(0, dets - 1)
    await_bytes(recv2.at[others, pl.ds(0, used2)], send_sems.at[1])
    await_bytes(recv3.at[others], send_sems.at[2])
    await_bytes(recv4.at[others], send_sems.at[3])
    await_bytes(recv_map.at[others, pl.ds(0, used_map)], send_sems.at[5])


INPUTS = 14


def per_device(
    patches, dets, tod_image, angles, pixel_offset, target_patch, target_block, noise_spectrum,
    residual, previous_rz, legendre, harmonic_filter,
):
    blocks, length = tod_image.shape[2:]
    vmem = pl.BlockSpec(memory_space=pltpu.VMEM)
    hbm = pl.BlockSpec(memory_space=pl.ANY)
    capacity = 2 * blocks // patches
    rows = residual.shape[1]
    modes_here = legendre.shape[0]
    operands = (
        tod_image[0, 0],
        jnp.asarray(fourier_matrix()),
        jnp.asarray(twiddle_rows()),
        noise_spectrum[0, 0],
        angles[0, 0],
        pixel_offset[0, 0],
        target_patch.reshape(1, blocks),
        target_block.reshape(1, blocks),
        residual[0].transpose(1, 0, 2),
        jnp.asarray(cycle_matrix(modes_here)),
        jnp.asarray(mode_rows(modes_here)),
        legendre,
        harmonic_filter,
        previous_rz.reshape(1, 1),
    )
    new, pre, beta = pl.pallas_call(
        functools.partial(step_kernel, patches, dets),
        out_shape=(
            jax.ShapeDtypeStruct((3, rows, 64), F32),
            jax.ShapeDtypeStruct((6, modes_here, 64), F32),
            jax.ShapeDtypeStruct((1, LANES), F32),
        ),
        in_specs=[hbm] * INPUTS,
        out_specs=(vmem, vmem, vmem),
        scratch_shapes=[pltpu.VMEM(a.shape, a.dtype) for a in operands]
        + [
            pltpu.VMEM((6, blocks, length), BF16),
            pltpu.VMEM((blocks, length), BF16),
            pltpu.VMEM((blocks, length), BF16),
            pltpu.VMEM((blocks, 256), F32),
            pltpu.VMEM((patches, 2 * capacity, LANES), F32),
            pltpu.VMEM((patches, 2 * capacity, LANES), F32),
            pltpu.VMEM((dets, 4 * modes_here, LANES), F32),
            pltpu.VMEM((dets, 4 * modes_here, LANES), F32),
            pltpu.VMEM((dets, 1, LANES), F32),
            pltpu.VMEM((dets, 1, LANES), F32),
            pltpu.VMEM((dets, 2 * rows, LANES), F32),
            pltpu.VMEM((dets, 2 * rows, LANES), F32),
            pltpu.VMEM((1, LANES), F32),
            pltpu.VMEM((dets, 1, LANES), F32),
            pltpu.VMEM((1, LANES), F32),
            pltpu.VMEM((patches, 1, LANES), F32),
            pltpu.SemaphoreType.DMA((INPUTS,)),
            pltpu.SemaphoreType.DMA((6,)),
            pltpu.SemaphoreType.DMA((6,)),
        ],
        compiler_params=pltpu.CompilerParams(
            collective_id=0, has_side_effects=True, vmem_limit_bytes=56 * 1024 * 1024
        ),
    )(*operands)
    return new.transpose(1, 0, 2)[None], pre.transpose(1, 0, 2)[None], beta[0, :1]


def solution(mesh):
    placed = (
        P("patch", "det", None, None),
        P("patch", "det", None, None),
        P("patch", "det", None, None),
        P("patch", "det", None, None),
        P("patch", "det", None),
        P("patch", "det", None, None),
        P("patch", "det", None, None),
        P(),
        P("det", None, None),
        P("det", None),
    )
    return jax.shard_map(
        functools.partial(per_device, mesh.shape["patch"], mesh.shape["det"]),
        mesh=mesh,
        in_specs=placed,
        out_specs=(P("patch", "det", None, None), P("patch", "det", None, None), P()),
        check_vma=False,
    )
```

time: 83.4 us -> 65.3 us (0.78)
  Pallas kernels: 74.5 us -> 60.5 us
  local copies, waits for them, and re-layouts: 6.01 us -> 2.01 us
    pallas_call x2 -> x1, Pallas kernels: 74.5 us -> 60.5 us  [per_device(): pl.pallas_call(functools.partial(step_kernel, patches, dets), out_shape=(...]
    unnamed x28 -> x8, local copies, waits for them, and re-layouts: 6.01 us -> 2.01 us
where the time goes in v2:
time: 65.3 us; the launch traced here: 65 us
  Pallas kernels  60.5 us (93%)
  between operations  2.46 us (4%)
  local copies, waits for them, and re-layouts  2.01 us (3%)
    pallas_call x1, Pallas kernels, per_device(): pl.pallas_call(functools.partial(step_kernel, patches, dets), out_shape=(...  60.5 us
    unnamed x8, local copies, waits for them, and re-layouts  2.01 us

profile of v2, /device:TPU:1, one launch (start us, length us, event | category | flops | bytes accessed | tf_op | source)
XLA Modules:
  0.0 65.0 jit_solution(12942564121673415308)
XLA Ops:
  1.3 60.5 %shard_map.157 = (f32[3,8,64]{2,1,0:T(8,128)}, f32[6,4,64]{2,1,0:T(4,128)}, f32[1,128]{1,0:T(1,128)}) custom-call(f32[128,1024]{1,0:T(8,128)} %bitcast.19, f32[256,256]{1,0:T(8,128)} %constant.8.clone.refs_1_, f32[8,128]{1,0:T(8,128)} %constant.9.clone.refs_2_, f32[4,513]{1,0:T(4,128)} %bitcast.25, f32[128,1024]{1,0:T(8,128)} %bitcast.20, ...), custom_call_target="tpu_custom_call" | custom-call | tf_op jit(solution)/shard_map/pallas_call | solution.py:583
  61.8 0.0 copy-start.1
  61.8 0.7 %copy-done.1 = f32[3,8,64]{2,1,0:T(8,128)S(1)} copy-done((f32[3,8,64]{2,1,0:T(8,128)S(1)}, f32[3,8,64]{2,1,0:T(8,128)}, u32[]{:S(2)}) %copy-start.1) | copy-done | bytes 6168
  62.5 0.0 copy-start
  62.5 0.6 copy.21
  63.1 0.1 copy-done
  63.2 0.0 copy-start.2
  63.2 0.6 copy.22
  63.8 0.0 copy-done.2
Async XLA Ops:
  61.8 0.7 %copy-start.1 = (f32[3,8,64]{2,1,0:T(8,128)S(1)}, f32[3,8,64]{2,1,0:T(8,128)}, u32[]{:S(2)}) copy-start(f32[3,8,64]{2,1,0:T(8,128)} %get-tuple-element.6) | copy-start | bytes 18436
  62.5 0.7 %copy-start = (f32[6,4,64]{2,1,0:T(4,128)S(1)}, f32[6,4,64]{2,1,0:T(4,128)}, u32[]{:S(2)}) copy-start(f32[6,4,64]{2,1,0:T(4,128)} %get-tuple-element.7) | copy-start | bytes 18436
  63.2 0.6 copy-start.2

commit v3 on v2

--- a/solution.py
+++ b/solution.py
@@ -54,7 +54,7 @@
     j = np.arange(LANES)
     angle = 2.0 * np.pi * (np.outer(j, j) % LANES) / LANES
     c, s = np.cos(angle), np.sin(angle)
-    return np.block([[c, -s], [s, c]]).astype(np.float32)
+    return np.concatenate([c, s], axis=1).astype(np.float32)
 
 
 def twiddle_rows():
@@ -118,9 +118,22 @@
 COS_POLY, SIN_POLY = fit_polys()
 
 
-def filter_blocks(x, spec_ref, table, tw):
+def noise_weights(own):
+    col = iota((1, 5 * LANES), 1)
+    k_of, j_of = col // LANES, col % LANES
+    order = k_of + RADIX * j_of
+    place = jnp.minimum(order, RADIX * LANES - order)
+    pick = (iota((512, 5 * LANES), 0) == place).astype(F32).astype(BF16)
+    parts = split3(own[:, :512])
+    weight = dot(parts[0], pick) + dot(parts[1], pick) + dot(parts[2], pick)
+    weight = weight + jnp.where(place == 512, own[:, 512:513], 0.0)
+    edge = (k_of == 0) | (k_of == 4)
+    return weight * jnp.where(edge, 1.0 / 1024.0, 2.0 / 1024.0)
+
+
+def filter_blocks(x, weight, table, tw):
     blocks = x.shape[0]
-    dets = spec_ref.shape[0]
+    dets = weight.shape[0]
     t = [x[:, i * LANES : (i + 1) * LANES] for i in range(RADIX)]
     a = [t[i] + t[i + 4] for i in range(4)]
     b = [t[i] - t[i + 4] for i in range(4)]
@@ -143,18 +156,6 @@
             rows.append(jnp.concatenate([re * c + im * s, im * c - re * s], axis=1))
     hi, lo = split2(jnp.concatenate(rows, axis=0))
     spectrum = dot(jnp.concatenate([hi, lo, hi], axis=1), table)
-
-    col = iota((1, 5 * LANES), 1)
-    k_of, j_of = col // LANES, col % LANES
-    order = k_of + RADIX * j_of
-    place = jnp.minimum(order, RADIX * LANES - order)
-    pick = (iota((512, 5 * LANES), 0) == place).astype(F32).astype(BF16)
-    own = spec_ref[...]
-    parts = split3(own[:, :512])
-    weight = dot(parts[0], pick) + dot(parts[1], pick) + dot(parts[2], pick)
-    weight = weight + jnp.where(place == 512, own[:, 512:513], 0.0)
-    edge = (k_of == 0) | (k_of == 4)
-    weight = weight * jnp.where(edge, 1.0 / 1024.0, 2.0 / 1024.0)
 
     per = blocks // dets
     scaled = []
@@ -202,14 +203,13 @@
     def one_group(g, carry):
         rows = pl.ds(pl.multiple_of(g * GROUP, GROUP), GROUP)
         low, high = low_ref[rows, :], high_ref[rows, :]
-        ones = jnp.concatenate(
-            [jnp.where(low == k, 1.0, 0.0).astype(BF16) for k in range(LOW)], axis=0
-        )
+        one, none = jnp.ones_like(low), jnp.zeros_like(low)
+        ones = jnp.concatenate([jnp.where(low == k, one, none) for k in range(LOW)], axis=0)
         masks = [high == k for k in range(HIGH)]
         values = []
         for comp in range(6):
             v = val_ref[comp, rows, :]
-            values += [jnp.where(masks[k], v, jnp.zeros_like(v)) for k in range(HIGH)]
+            values += [jnp.where(masks[k], v, none) for k in range(HIGH)]
         got = dot_nt(jnp.concatenate(values, axis=0), ones)
         half = 3 * HIGH * GROUP
         got = got[:half, :] + got[half:, :]
@@ -228,7 +228,7 @@
             binned_ref[rows, h * LANES : (h + 1) * LANES] = acc
         return carry
 
-    lax.fori_loop(0, blocks // GROUP, one_group, 0)
+    lax.fori_loop(0, blocks // GROUP, one_group, 0, unroll=blocks // GROUP)
     turned = iota((blocks, LANES), 0)
     turned = turned + (turned >> 3 & 1)
     halves = []
@@ -240,12 +240,10 @@
     return jnp.concatenate(halves, axis=1)
 
 
-def route(patches, binned, curvature, patch_row, block_row, order):
-    blocks = binned.shape[0]
+def plan_route(patches, patch_row, block_row):
+    blocks = patch_row.shape[1]
     capacity = 2 * blocks // patches
     quarter = capacity // 2
-    hi, lo = split2(binned)
-    moved = dot(jnp.concatenate([hi, lo], axis=1), jnp.concatenate([order, order], axis=0))
     patch_row = patch_row.astype(F32)
     block_row = block_row.astype(F32)
     patch_col = jnp.broadcast_to(patch_row, (blocks, blocks)).T
@@ -265,37 +263,87 @@
     select = choose(own == place)
     select_a = choose((own == place) & first_half)
     select_b = choose((own + quarter == place) & first_half)
+    named = jnp.where((row // capacity).astype(F32) == patch_row, block_row + 1.0, 0.0)
+    slot_lane = (iota((blocks, LANES), 1) % capacity).astype(F32)
+    labels = dot(named.astype(BF16), choose(slot_col == slot_lane))
+    return (
+        jnp.concatenate([select, select], axis=1),
+        jnp.concatenate([select_a, select_a, select_b, select_b], axis=1),
+        labels,
+    )
+
+
+def route(patches, binned, curvature, order, selects):
+    front_select, back_select, labels = selects
+    capacity = 2 * binned.shape[0] // patches
+    hi, lo = split2(binned)
+    moved = dot(jnp.concatenate([hi, lo], axis=1), jnp.concatenate([order, order], axis=0))
     hi, lo = split2(moved[:, :LANES])
-    front = dot(jnp.concatenate([select, select], axis=1), jnp.concatenate([hi, lo], axis=0))
+    front = dot(front_select, jnp.concatenate([hi, lo], axis=0))
     back = moved[:, LANES:]
     hi, lo = split2(back)
     hi2, lo2 = split2(pltpu.roll(back, 64, 1))
-    back = dot(
-        jnp.concatenate([select_a, select_a, select_b, select_b], axis=1),
-        jnp.concatenate([hi, lo, hi2, lo2], axis=0),
-    )
-    named = jnp.where((row // capacity).astype(F32) == patch_row, block_row + 1.0, 0.0)
-    slot_lane = (iota((blocks, LANES), 1) % capacity).astype(F32)
-    labels = dot(named.astype(BF16), choose(slot_col == slot_lane))
+    back = dot(back_select, jnp.concatenate([hi, lo, hi2, lo2], axis=0))
     labels = jnp.where(iota(labels.shape, 1) < 64, labels, curvature)
-    back = jnp.where(iota(back.shape, 0) % capacity == quarter, labels, back)
+    back = jnp.where(iota(back.shape, 0) % capacity == capacity // 2, labels, back)
     return front, back
 
 
-def start_exchange(axis, count, me, send_at, recv_at, send_sem, recv_sem):
-    def one(step, carry):
-        peer = lax.rem(me + step, count)
+class Place:
+    def __init__(self, patches, dets):
+        self.tall, self.wide = patches // 4, dets // 4
+        self.patch, self.det = lax.axis_index("patch"), lax.axis_index("det")
+        self.y, corner = lax.div(self.patch, 4), lax.rem(self.patch, 4)
+        far, core = lax.div(corner, 2), lax.rem(corner, 2)
+        self.x, near = lax.div(self.det, 4), lax.rem(self.det, 4)
+        across = self.x * 4 + lax.rem(near + 2, 4)
+        self.patch_inner = [
+            ((1 - far) * 2 + (1 - core), across),
+            ((1 - far) * 2 + core, across),
+            (far * 2 + (1 - core), self.det),
+            (corner, self.det),
+        ]
+        self.det_inner = [lax.rem(near + step, 4) for step in (2, 1, 3, 0)]
+
+    def each_patch(self, act):
+        def lines(outer, count):
+            turned = self.y + self.tall // 2 + (1 - 2 * lax.rem(outer, 2)) * lax.div(outer + 1, 2)
+            base = lax.rem(turned, self.tall) * 4
+            for corner, det in self.patch_inner[:count]:
+                act(base + corner, det, base + corner)
+
+        self.walk(self.tall, lines)
+
+    def each_det(self, act):
+        def lines(outer, count):
+            turned = self.x + self.wide // 2 + (1 - 2 * lax.rem(outer, 2)) * lax.div(outer + 1, 2)
+            base = lax.rem(turned, self.wide) * 4
+            for near in self.det_inner[:count]:
+                act(self.patch, base + near, base + near)
+
+        self.walk(self.wide, lines)
+
+    def walk(self, count, lines):
+        def one(outer, carry):
+            lines(outer, 4)
+            return carry
+
+        lax.fori_loop(0, count - 1, one, 0)
+        lines(jnp.int32(count - 1), 3)
+
+
+def start_exchange(each, me, send_at, recv_at, send_sem, recv_sem):
+    def act(patch, det, index):
         pltpu.make_async_remote_copy(
-            src_ref=send_at(peer),
+            src_ref=send_at(index),
             dst_ref=recv_at(me),
             send_sem=send_sem,
             recv_sem=recv_sem,
-            device_id={axis: peer},
+            device_id=(patch, det),
             device_id_type=MESH,
         ).start()
-        return carry
-
-    lax.fori_loop(1, count, one, 0)
+
+    each(act)
     pltpu.make_async_copy(send_at(me), recv_at(me), recv_sem).start()
 
 
@@ -329,44 +377,52 @@
         send1, recv1, send2, recv2, send3, recv3, send_map, recv_map, send4, recv4, send5, recv5,
         in_sems, send_sems, recv_sems,
     ) = refs
-    my_patch, my_det = lax.axis_index("patch"), lax.axis_index("det")
+    place = Place(patches, dets)
+    over_patch = (place.each_patch, place.patch)
+    over_det = (place.each_det, place.det)
     fetches = [
         pltpu.make_async_copy(src, dst, in_sems.at[i]) for i, (src, dst) in enumerate(zip(hbm, held))
     ]
-    for fetch in fetches:
+    for fetch in fetches[:FIRST]:
         fetch.start()
     barrier = pltpu.get_barrier_semaphore()
 
-    def greet(axis, count, me):
-        def one(step, carry):
-            pl.semaphore_signal(
-                barrier, inc=1, device_id={axis: lax.rem(me + step, count)}, device_id_type=MESH
-            )
-            return carry
-
-        lax.fori_loop(1, count, one, 0)
-
-    greet("patch", patches, my_patch)
-    greet("det", dets, my_det)
+    def greet(patch, det, index):
+        pl.semaphore_signal(barrier, inc=1, device_id=(patch, det), device_id_type=MESH)
+
+    place.each_patch(greet)
+    place.each_det(greet)
     (
-        x_ref, table_ref, tw_ref, spec_ref, angle_ref, offset_ref, patch_ref, block_ref,
+        x_ref, table_ref, tw_ref, spec_ref, patch_ref, block_ref, angle_ref, offset_ref,
         res_ref, cycle_ref, modes_ref, leg_ref, filt_ref, rz_ref,
     ) = held
 
-    for fetch in fetches[:4]:
+    for fetch in fetches[3:6]:
         fetch.wait()
+    selects = plan_route(patches, patch_ref[...], block_ref[...])
+    order = pixel_order()
+    weight = noise_weights(spec_ref[...])
+    for fetch in fetches[:3]:
+        fetch.wait()
+    for fetch in fetches[FIRST:]:
+        fetch.start()
     x = x_ref[...]
-    filtered = filter_blocks(x, spec_ref, stack_table(table_ref[...]), tw_ref[...])
+    waves = table_ref[...]
+    swapped = jnp.concatenate([waves[:, LANES:], waves[:, :LANES]], axis=1)
+    signed = jnp.where(iota(waves.shape, 1) < LANES, waves, -waves)
+    table = stack_table(jnp.concatenate([signed, swapped], axis=0))
+    filtered = filter_blocks(x, weight, table, tw_ref[...])
     total = jnp.zeros((x.shape[0], LANES), F32)
     for i in range(RADIX):
         total = total + x[:, i * LANES : (i + 1) * LANES] * filtered[i]
     curvature = jnp.sum(jnp.sum(total, axis=0, keepdims=True), axis=1, keepdims=True)
-    for fetch in fetches[4:]:
+    for fetch in fetches[FIRST : FIRST + 2]:
         fetch.wait()
     binned = bin_blocks(filtered, angle_ref, offset_ref, val_ref, low_ref, high_ref, binned_ref)
-    front, back = route(
-        patches, binned, curvature, patch_ref[...], block_ref[...], pixel_order()
-    )
+    front, back = route(patches, binned, curvature, order, selects)
+    def drain(count, ref, index):
+        await_bytes(ref.at[pl.ds(0, count - 1)], send_sems.at[index])
+
     capacity = front.shape[0] // patches
     half = capacity // 2
     send1[:, :capacity, :] = front.reshape(patches, capacity, LANES)
@@ -374,11 +430,13 @@
     pl.semaphore_wait(barrier, patches + dets - 2)
     used1 = capacity + half + 1
     start_exchange(
-        "patch", patches, my_patch,
+        *over_patch,
         lambda p: send1.at[p, pl.ds(0, used1)], lambda p: recv1.at[p, pl.ds(0, used1)],
         send_sems.at[0], recv_sems.at[0],
     )
 
+    for fetch in fetches[FIRST + 2 :]:
+        fetch.wait()
     rows = res_ref.shape[1]
     modes_here = LANES // dets
     lines = []
@@ -407,7 +465,7 @@
     for d in range(dets):
         send3[d] = message[d : d + 1, :]
     start_exchange(
-        "det", dets, my_det, lambda d: send3.at[d], lambda d: recv3.at[d],
+        *over_det, lambda d: send3.at[d], lambda d: recv3.at[d],
         send_sems.at[2], recv_sems.at[2],
     )
 
@@ -475,7 +533,7 @@
     send2[:, group:, :] = modes1.reshape(dets, group, LANES)
     used2 = group + modes_here + 1
     start_exchange(
-        "det", dets, my_det,
+        *over_det,
         lambda d: send2.at[d, pl.ds(0, used2)], lambda d: recv2.at[d, pl.ds(0, used2)],
         send_sems.at[1], recv_sems.at[1],
     )
@@ -484,20 +542,14 @@
     used_map = rows + rows // 2
     send_map[:, :rows, :] = map0.reshape(dets, rows, LANES)
     send_map[:, rows:, :] = fold_rows(map1, rows // 2).reshape(dets, rows, LANES)
-    start_exchange(
-        "det", dets, my_det,
-        lambda d: send_map.at[d, pl.ds(0, used_map)], lambda d: recv_map.at[d, pl.ds(0, used_map)],
-        send_sems.at[5], recv_sems.at[5],
-    )
-
     await_bytes(recv3, recv_sems.at[2])
     cycles = recv3[...].reshape(dets, LANES)
     cycles = jnp.concatenate([cycles, pltpu.roll(cycles, 64, 1)], axis=0)
     cycles = jnp.concatenate([cycles, jnp.zeros((LANES - 2 * dets, LANES), F32)], axis=0).T
     columns = 6 * modes_here
     ring_of = iota((2 * dets, 2 * dets), 0)
-    place = iota((2 * dets, 2 * dets), 1)
-    order = (ring_of == 2 * (place % dets) + place // dets).astype(F32).astype(BF16)
+    column = iota((2 * dets, 2 * dets), 1)
+    order = (ring_of == 2 * (column % dets) + column // dets).astype(F32).astype(BF16)
     legendre = leg_ref[...].reshape(modes_here * 64, 2 * dets)
     a, b, c = split3(legendre)
     coef_old = legendre_columns(
@@ -519,10 +571,23 @@
     rz = jnp.sum(jnp.sum(pre * coef, axis=0, keepdims=True), axis=1, keepdims=True)
     send4[...] = jnp.broadcast_to(rz, (1, LANES))
     start_exchange(
-        "det", dets, my_det, lambda d: send4, lambda d: recv4.at[d], send_sems.at[3], recv_sems.at[3]
+        *over_det, lambda d: send4, lambda d: recv4.at[d], send_sems.at[3], recv_sems.at[3]
+    )
+    drain(dets, recv2.at[:, pl.ds(0, used2)], 1)
+    start_exchange(
+        *over_det,
+        lambda d: send_map.at[d, pl.ds(0, used_map)], lambda d: recv_map.at[d, pl.ds(0, used_map)],
+        send_sems.at[5], recv_sems.at[5],
     )
     for c in range(6):
         pre_ref[c] = pre[c * modes_here : (c + 1) * modes_here, :]
+
+    await_bytes(recv4, recv_sems.at[3])
+    send5[...] = jnp.sum(recv4[...], axis=0)
+    start_exchange(
+        *over_patch, lambda p: send5, lambda p: recv5.at[p],
+        send_sems.at[4], recv_sems.at[4],
+    )
     await_bytes(recv_map.at[:, pl.ds(0, used_map)], recv_sems.at[5])
     image0 = jnp.sum(recv_map[:, :rows, :], axis=0)
     image1 = jnp.sum(recv_map[:, rows:, :], axis=0)
@@ -532,26 +597,24 @@
     new_ref[1] = res_ref[1] - step_size * pltpu.roll(image0, 64, 1)[:, :64]
     new_ref[2] = res_ref[2] - step_size * image1[:, :64]
 
-    await_bytes(recv4, recv_sems.at[3])
-    send5[...] = jnp.sum(recv4[...], axis=0)
-    start_exchange(
-        "patch", patches, my_patch, lambda p: send5, lambda p: recv5.at[p],
-        send_sems.at[4], recv_sems.at[4],
-    )
     await_bytes(recv5, recv_sems.at[4])
     beta_ref[...] = jnp.sum(recv5[...], axis=0) / rz_before
 
-    others = pl.ds(0, patches - 1)
-    await_bytes(recv1.at[others, pl.ds(0, used1)], send_sems.at[0])
-    await_bytes(recv5.at[others], send_sems.at[4])
-    others = pl.ds(0, dets - 1)
-    await_bytes(recv2.at[others, pl.ds(0, used2)], send_sems.at[1])
-    await_bytes(recv3.at[others], send_sems.at[2])
-    await_bytes(recv4.at[others], send_sems.at[3])
-    await_bytes(recv_map.at[others, pl.ds(0, used_map)], send_sems.at[5])
+    drain(patches, recv1.at[:, pl.ds(0, used1)], 0)
+    drain(dets, recv3, 2)
+    drain(dets, recv4, 3)
+    drain(patches, recv5, 4)
+    drain(dets, recv_map.at[:, pl.ds(0, used_map)], 5)
+
+
+def finish_kernel(new_in, pre_in, beta_in, new_ref, pre_ref, beta_ref):
+    new_ref[...] = new_in[...]
+    pre_ref[...] = pre_in[...]
+    beta_ref[...] = beta_in[:, :1]
 
 
 INPUTS = 14
+FIRST = 6
 
 
 def per_device(
@@ -569,10 +632,10 @@
         jnp.asarray(fourier_matrix()),
         jnp.asarray(twiddle_rows()),
         noise_spectrum[0, 0],
+        target_patch.reshape(1, blocks),
+        target_block.reshape(1, blocks),
         angles[0, 0],
         pixel_offset[0, 0],
-        target_patch.reshape(1, blocks),
-        target_block.reshape(1, blocks),
         residual[0].transpose(1, 0, 2),
         jnp.asarray(cycle_matrix(modes_here)),
         jnp.asarray(mode_rows(modes_here)),
@@ -583,9 +646,9 @@
     new, pre, beta = pl.pallas_call(
         functools.partial(step_kernel, patches, dets),
         out_shape=(
-            jax.ShapeDtypeStruct((3, rows, 64), F32),
-            jax.ShapeDtypeStruct((6, modes_here, 64), F32),
-            jax.ShapeDtypeStruct((1, LANES), F32),
+            pltpu.VMEM((3, rows, 64), F32),
+            pltpu.VMEM((6, modes_here, 64), F32),
+            pltpu.VMEM((1, LANES), F32),
         ),
         in_specs=[hbm] * INPUTS,
         out_specs=(vmem, vmem, vmem),
@@ -615,7 +678,17 @@
             collective_id=0, has_side_effects=True, vmem_limit_bytes=56 * 1024 * 1024
         ),
     )(*operands)
-    return new.transpose(1, 0, 2)[None], pre.transpose(1, 0, 2)[None], beta[0, :1]
+    new, pre, beta = pl.pallas_call(
+        finish_kernel,
+        out_shape=(
+            jax.ShapeDtypeStruct(new.shape, F32),
+            jax.ShapeDtypeStruct(pre.shape, F32),
+            jax.ShapeDtypeStruct((1, 1), F32),
+        ),
+        in_specs=[vmem] * 3,
+        out_specs=(vmem,) * 3,
+    )(new, pre, beta)
+    return new.transpose(1, 0, 2)[None], pre.transpose(1, 0, 2)[None], beta.reshape(1)
 
 
 def solution(mesh):

time: 65.3 us -> 59 us (0.904)
  Pallas kernels: 60.5 us -> 55.7 us
  between operations: 2.46 us -> 1.3 us
    pallas_call x1, Pallas kernels: 60.5 us -> 54.3 us  [per_device(): pl.pallas_call(functools.partial(step_kernel, patches, dets), out_shape=(...]
    pallas_call x0 -> x1, Pallas kernels: none -> 1.33 us  [per_device(): pl.pallas_call(finish_kernel, out_shape=(jax.ShapeDtypeStruct(new.shape,...]
    unnamed x8 -> x6, local copies, waits for them, and re-layouts: 2.01 us -> 1.78 us
where the time goes in v3:
time: 59 us; the launch traced here: 58.8 us
  Pallas kernels  55.7 us (94%)
  local copies, waits for them, and re-layouts  1.78 us (3%)
  between operations  1.3 us (2%)
    pallas_call x1, Pallas kernels, per_device(): pl.pallas_call(functools.partial(step_kernel, patches, dets), out_shape=(...  54.3 us
    unnamed x6, local copies, waits for them, and re-layouts  1.78 us
    pallas_call x1, Pallas kernels, per_device(): pl.pallas_call(finish_kernel, out_shape=(jax.ShapeDtypeStruct(new.shape,...  1.33 us

profile of v3, /device:TPU:1, one launch (start us, length us, event | category | flops | bytes accessed | tf_op | source)
XLA Modules:
  0.0 58.8 jit_solution(13524671345774376505)
XLA Ops:
  1.3 54.3 %shard_map.157 = (f32[3,8,64]{2,1,0:T(8,128)S(1)}, f32[6,4,64]{2,1,0:T(4,128)S(1)}, f32[1,128]{1,0:T(1,128)S(1)}) custom-call(f32[128,1024]{1,0:T(8,128)} %bitcast.18, f32[128,256]{1,0:T(8,128)} %constant.8.clone.refs_1_, f32[8,128]{1,0:T(8,128)} %constant.9.clone.refs_2_, f32[4,513]{1,0:T(4,128)} %bitcast.22, s32[1,128]{1,0:T(1,128)} %bitcast.23, ...), custom_call_target="tpu_custom_call" | custom-call | tf_op jit(solution)/shard_map/pallas_call | solution.py:646
  55.6 0.0 copy-start
  55.6 0.6 %copy-done = f32[3,8,64]{2,1,0:T(8,128)} copy-done((f32[3,8,64]{2,1,0:T(8,128)}, f32[3,8,64]{2,1,0:T(8,128)S(1)}, u32[]{:S(2)}) %copy-start) | copy-done | bytes 6168
  56.2 0.0 copy-start.1
  56.2 0.6 %copy-done.1 = f32[6,4,64]{2,1,0:T(4,128)} copy-done((f32[6,4,64]{2,1,0:T(4,128)}, f32[6,4,64]{2,1,0:T(4,128)S(1)}, u32[]{:S(2)}) %copy-start.1) | copy-done | bytes 6168
  56.8 0.0 copy-start.2
  56.8 0.6 %copy-done.2 = f32[1,128]{1,0:T(1,128)} copy-done((f32[1,128]{1,0:T(1,128)}, f32[1,128]{1,0:T(1,128)S(1)}, u32[]{:S(2)}) %copy-start.2) | copy-done | bytes 536
  57.4 1.3 %shard_map.158 = (f32[3,8,64]{2,1,0:T(8,128)}, f32[6,4,64]{2,1,0:T(4,128)}, f32[1,1]{1,0:T(1,128)}) custom-call(f32[3,8,64]{2,1,0:T(8,128)} %copy-done, f32[6,4,64]{2,1,0:T(4,128)} %copy-done.1, f32[1,128]{1,0:T(1,128)} %copy-done.2), custom_call_target="tpu_custom_call" | custom-call | tf_op jit(solution)/shard_map/pallas_call | solution.py:681
Async XLA Ops:
  55.6 0.6 %copy-start = (f32[3,8,64]{2,1,0:T(8,128)}, f32[3,8,64]{2,1,0:T(8,128)S(1)}, u32[]{:S(2)}) copy-start(f32[3,8,64]{2,1,0:T(8,128)S(1)} %get-tuple-element.9.new_in) | copy-start | bytes 18436
  56.2 0.6 %copy-start.1 = (f32[6,4,64]{2,1,0:T(4,128)}, f32[6,4,64]{2,1,0:T(4,128)S(1)}, u32[]{:S(2)}) copy-start(f32[6,4,64]{2,1,0:T(4,128)S(1)} %get-tuple-element.10.pre_in) | copy-start | bytes 18436
  56.8 0.6 %copy-start.2 = (f32[1,128]{1,0:T(1,128)}, f32[1,128]{1,0:T(1,128)S(1)}, u32[]{:S(2)}) copy-start(f32[1,128]{1,0:T(1,128)S(1)} %get-tuple-element.11.beta_in) | copy-start | bytes 1540

commit v4 on v3

--- a/solution.py
+++ b/solution.py
@@ -124,8 +124,10 @@
     order = k_of + RADIX * j_of
     place = jnp.minimum(order, RADIX * LANES - order)
     pick = (iota((512, 5 * LANES), 0) == place).astype(F32).astype(BF16)
-    parts = split3(own[:, :512])
-    weight = dot(parts[0], pick) + dot(parts[1], pick) + dot(parts[2], pick)
+    dets = own.shape[0]
+    parts = jnp.concatenate([part.astype(F32) for part in split3(own[:, :512])], axis=0)
+    weight = dot(parts.astype(BF16), pick)
+    weight = weight[:dets] + weight[dets : 2 * dets] + weight[2 * dets :]
     weight = weight + jnp.where(place == 512, own[:, 512:513], 0.0)
     edge = (k_of == 0) | (k_of == 4)
     return weight * jnp.where(edge, 1.0 / 1024.0, 2.0 / 1024.0)
@@ -404,7 +406,7 @@
     weight = noise_weights(spec_ref[...])
     for fetch in fetches[:3]:
         fetch.wait()
-    for fetch in fetches[FIRST:]:
+    for fetch in fetches[FIRST : FIRST + 2]:
         fetch.start()
     x = x_ref[...]
     waves = table_ref[...]
@@ -418,6 +420,8 @@
     curvature = jnp.sum(jnp.sum(total, axis=0, keepdims=True), axis=1, keepdims=True)
     for fetch in fetches[FIRST : FIRST + 2]:
         fetch.wait()
+    for fetch in fetches[FIRST + 2 :]:
+        fetch.start()
     binned = bin_blocks(filtered, angle_ref, offset_ref, val_ref, low_ref, high_ref, binned_ref)
     front, back = route(patches, binned, curvature, order, selects)
     def drain(count, ref, index):
@@ -556,7 +560,7 @@
         cycles[: columns + 8, : 2 * dets], dot(a, order) + dot(b, order) + dot(c, order), modes_here
     )
     weight = jnp.concatenate([filt_ref[...]] * 6, axis=0)
-    rz_before = rz_ref[...]
+    rz_before = rz_ref[0]
 
     await_bytes(recv2.at[:, pl.ds(0, used2)], recv_sems.at[1])
     sum0 = jnp.sum(recv2[:, :group, :], axis=0)
@@ -641,7 +645,7 @@
         jnp.asarray(mode_rows(modes_here)),
         legendre,
         harmonic_filter,
-        previous_rz.reshape(1, 1),
+        previous_rz,
     )
     new, pre, beta = pl.pallas_call(
         functools.partial(step_kernel, patches, dets),
@@ -652,7 +656,8 @@
         ),
         in_specs=[hbm] * INPUTS,
         out_specs=(vmem, vmem, vmem),
-        scratch_shapes=[pltpu.VMEM(a.shape, a.dtype) for a in operands]
+        scratch_shapes=[pltpu.VMEM(a.shape, a.dtype) for a in operands[:-1]]
+        + [pltpu.SMEM((1,), F32)]
         + [
             pltpu.VMEM((6, blocks, length), BF16),
             pltpu.VMEM((blocks, length), BF16),
@@ -687,6 +692,7 @@
         ),
         in_specs=[vmem] * 3,
         out_specs=(vmem,) * 3,
+        compiler_params=pltpu.CompilerParams(vmem_limit_bytes=1024 * 1024),
     )(new, pre, beta)
     return new.transpose(1, 0, 2)[None], pre.transpose(1, 0, 2)[None], beta.reshape(1)
 

time: 59 us -> 56 us (0.949)
  local copies, waits for them, and re-layouts: 1.78 us -> 0 us
  Pallas kernels: 55.7 us -> 54.6 us
    unnamed x6 -> x0, local copies, waits for them, and re-layouts: 1.78 us -> none
    pallas_call x1, Pallas kernels: 1.33 us -> 0.61 us  [per_device(): pl.pallas_call(finish_kernel, out_shape=(jax.ShapeDtypeStruct(new.shape,...]
where the time goes in v4:
time: 56 us; the launch traced here: 55.8 us
  Pallas kernels  54.6 us (98%)
  between operations  1.29 us (2%)
    pallas_call x1, Pallas kernels, per_device(): pl.pallas_call(functools.partial(step_kernel, patches, dets), out_shape=(...  53.9 us

profile of v4, /device:TPU:1, one launch (start us, length us, event | category | flops | bytes accessed | tf_op | source)
XLA Modules:
  0.0 55.8 jit_solution(6431880206854515320)
XLA Ops:
  1.3 53.9 %shard_map.157 = (f32[3,8,64]{2,1,0:T(8,128)S(1)}, f32[6,4,64]{2,1,0:T(4,128)S(1)}, f32[1,128]{1,0:T(1,128)S(1)}) custom-call(f32[128,1024]{1,0:T(8,128)} %bitcast.16, f32[128,256]{1,0:T(8,128)} %constant.8.clone.refs_1_, f32[8,128]{1,0:T(8,128)} %constant.9.clone.refs_2_, f32[4,513]{1,0:T(4,128)} %bitcast.20, s32[1,128]{1,0:T(1,128)} %bitcast.21, ...), custom_call_target="tpu_custom_call" | custom-call | tf_op jit(solution)/shard_map/pallas_call | solution.py:650
  55.2 0.6 %shard_map.158 = (f32[3,8,64]{2,1,0:T(8,128)}, f32[6,4,64]{2,1,0:T(4,128)}, f32[1,1]{1,0:T(1,128)}) custom-call(f32[3,8,64]{2,1,0:T(8,128)S(1)} %get-tuple-element.9.new_in, f32[6,4,64]{2,1,0:T(4,128)S(1)} %get-tuple-element.10.pre_in, f32[1,128]{1,0:T(1,128)S(1)} %get-tuple-element.11.beta_in), custom_call_target="tpu_custom_call" | custom-call | tf_op jit(solution)/shard_map/pallas_call | solution.py:686

commit v5 on v4

--- a/solution.py
+++ b/solution.py
@@ -360,7 +360,7 @@
 
 def legendre_columns(columns, legendre, modes_here):
     hi, lo = split2(columns)
-    leg_hi, leg_lo = split2(legendre)
+    leg_hi, leg_lo = legendre
     product = dot_nt(hi, leg_hi) + dot_nt(lo, leg_hi) + dot_nt(hi, leg_lo)
     rows = 6 * modes_here
     mode_of = iota((rows, 64), 0) % modes_here
@@ -404,10 +404,10 @@
     selects = plan_route(patches, patch_ref[...], block_ref[...])
     order = pixel_order()
     weight = noise_weights(spec_ref[...])
+    for fetch in fetches[FIRST : FIRST + 2]:
+        fetch.start()
     for fetch in fetches[:3]:
         fetch.wait()
-    for fetch in fetches[FIRST : FIRST + 2]:
-        fetch.start()
     x = x_ref[...]
     waves = table_ref[...]
     swapped = jnp.concatenate([waves[:, LANES:], waves[:, :LANES]], axis=1)
@@ -473,6 +473,10 @@
         send_sems.at[2], recv_sems.at[2],
     )
 
+    mode_hi, mode_lo = split2(modes_ref[...])
+    mode_table = jnp.concatenate([mode_hi, mode_lo, mode_hi], axis=1)
+    row = iota((256, patches * capacity), 0)
+    interleaved = (row % 64 * 4 + row // 64 + 1).astype(F32)
     await_bytes(recv1.at[:, pl.ds(0, used1)], recv_sems.at[0])
     got0 = recv1[:, :capacity, :].reshape(patches * capacity, LANES)
     got1 = recv1[:, capacity:, :]
@@ -507,8 +511,7 @@
             dot(jnp.concatenate([hit, hit, hit_b, hit_b], axis=1), rhs1),
         )
 
-    row = iota((256, patches * capacity), 0)
-    map0, map1 = spread((row % 64 * 4 + row // 64 + 1).astype(F32))
+    map0, map1 = spread(interleaved)
     left = iota((64, LANES), 1) < 64
     fields = []
     for s in range(3):
@@ -523,9 +526,8 @@
                 tiles.append(jnp.where(left, a, pltpu.roll(b, 64, 1)))
         fields.append(jnp.concatenate(tiles, axis=1))
     hi, lo = split2(jnp.concatenate(fields, axis=0))
-    mode_hi, mode_lo = split2(modes_ref[...])
     modes = dot_nt(
-        jnp.concatenate([mode_hi, mode_lo, mode_hi], axis=1),
+        mode_table,
         jnp.concatenate([hi, hi, lo], axis=1),
     )
     group = 2 * modes_here
@@ -557,8 +559,11 @@
     legendre = leg_ref[...].reshape(modes_here * 64, 2 * dets)
     a, b, c = split3(legendre)
     coef_old = legendre_columns(
-        cycles[: columns + 8, : 2 * dets], dot(a, order) + dot(b, order) + dot(c, order), modes_here
-    )
+        cycles[: columns + 8, : 2 * dets],
+        split2(dot(a, order) + dot(b, order) + dot(c, order)),
+        modes_here,
+    )
+    legendre = split2(legendre)
     weight = jnp.concatenate([filt_ref[...]] * 6, axis=0)
     rz_before = rz_ref[0]
 

time: 56 us -> 56.4 us (level)
  no operation moved by 1% of the time
where the time goes in v5:
time: 56.4 us; the launch traced here: 56.2 us
  Pallas kernels  54.9 us (97%)
  between operations  1.29 us (2%)
    pallas_call x1, Pallas kernels, per_device(): pl.pallas_call(functools.partial(step_kernel, patches, dets), out_shape=(...  54.3 us

profile of v5, /device:TPU:1, one launch (start us, length us, event | category | flops | bytes accessed | tf_op | source)
XLA Modules:
  0.0 56.2 jit_solution(13224120503508787274)
XLA Ops:
  1.3 54.3 %shard_map.157 = (f32[3,8,64]{2,1,0:T(8,128)S(1)}, f32[6,4,64]{2,1,0:T(4,128)S(1)}, f32[1,128]{1,0:T(1,128)S(1)}) custom-call(f32[128,1024]{1,0:T(8,128)} %bitcast.16, f32[128,256]{1,0:T(8,128)} %constant.8.clone.refs_1_, f32[8,128]{1,0:T(8,128)} %constant.9.clone.refs_2_, f32[4,513]{1,0:T(4,128)} %bitcast.20, s32[1,128]{1,0:T(1,128)} %bitcast.21, ...), custom_call_target="tpu_custom_call" | custom-call | tf_op jit(solution)/shard_map/pallas_call | solution.py:655
  55.6 0.6 %shard_map.158 = (f32[3,8,64]{2,1,0:T(8,128)}, f32[6,4,64]{2,1,0:T(4,128)}, f32[1,1]{1,0:T(1,128)}) custom-call(f32[3,8,64]{2,1,0:T(8,128)S(1)} %get-tuple-element.9.new_in, f32[6,4,64]{2,1,0:T(4,128)S(1)} %get-tuple-element.10.pre_in, f32[1,128]{1,0:T(1,128)S(1)} %get-tuple-element.11.beta_in), custom_call_target="tpu_custom_call" | custom-call | tf_op jit(solution)/shard_map/pallas_call | solution.py:691
